TPU v7x, 128 devices: a whole 4x4x4 slice. The times are simulated.
128 devices in a mesh: col: 8 (over y_hi, x), row: 16 (over y_lo, z, core).
Axes of the slice: x: 4, y: 4 (y_hi: 2, y_lo: 2; y = y_hi * 2 + y_lo), z: 4, core: 2. Of those that a mesh axis runs over, the one named last changes fastest.
Arguments:
- inputs: bfloat16 [16384, 4096], P(('col', 'row')), may hold values from -6 to 6
- leaf_maps: bfloat16 [16384, 4096], P(('col', 'row')), may hold values from -0.75 to 0.75
- expand_maps: bfloat16 [16384, 4096], P(('col', 'row')), may hold values from -0.75 to 0.75
- patterns: int32 [14, 16384], replicated, may hold values from 0 to 63
- translations: bfloat16 [64, 64, 128], replicated, may hold values from -0.5 to 0.5
Outputs:
- applied: bfloat16 [16384, 4096], P(('col', 'row'))
All inputs are finite; a program needn't handle non-finite values.
Results may differ from a plain program's by a relative error of at most 0.029.
Values may be sent and summed in bfloat16 or wider, within the bound.
No kernel may reach another device: no remote copies, remote signals or barrier semaphores. Data moves between devices by JAX's collectives and lax.ppermute only.
A program may use at most 128 MiB of HBM per device.

v0:
```python
import jax
import jax.numpy as jnp
from jax import lax
from jax.sharding import PartitionSpec as P

LEAF = 64
RANK = 64
VECS = 64


def swapped(array, axis, stride):
    return lax.ppermute(array, axis, [(i, i ^ 1 << stride) for i in range(lax.axis_size(axis))])


def pair_flip(values, level_bit):
    count = values.shape[0]
    shaped = values.reshape((count >> level_bit + 1, 2, 1 << level_bit) + values.shape[1:])
    return jnp.flip(shaped, 1).reshape(values.shape)


def combine(own, partner, chosen, translations):
    count = own.shape[0]
    dict_count = translations.shape[0]
    selector = (chosen[:, None] == jnp.arange(dict_count, dtype=jnp.int32)[None, :]).astype(
        jnp.bfloat16
    )
    table = translations.reshape(dict_count, RANK * 2 * RANK)
    mats = jnp.dot(selector, table, preferred_element_type=jnp.float32).astype(jnp.bfloat16)
    mats = mats.reshape(count, RANK, 2 * RANK)
    stacked = jnp.concatenate([own, partner], axis=1)
    summed = jnp.einsum("brt,btk->brk", mats, stacked, preferred_element_type=jnp.float32)
    return summed.astype(jnp.bfloat16)


def local(inputs, leaf_maps, expand_maps, patterns, translations):
    boxes_here = inputs.shape[0]
    col_count = lax.axis_size("col")
    row_count = lax.axis_size("row")
    col_bits = col_count.bit_length() - 1
    row_bits = row_count.bit_length() - 1
    local_bits = boxes_here.bit_length() - 1
    col_place = lax.axis_index("col")
    row_place = lax.axis_index("row")
    first_box = (col_place * row_count + row_place) * boxes_here

    def own_pattern(level):
        return lax.dynamic_slice_in_dim(patterns[level], first_box, boxes_here)

    source = inputs.reshape(boxes_here, LEAF, VECS)
    compress = leaf_maps.reshape(boxes_here, LEAF, RANK)
    state = jnp.einsum("jlr,jlk->jrk", compress, source, preferred_element_type=jnp.float32).astype(
        jnp.bfloat16
    )
    for level_bit in range(col_bits):
        partner = swapped(state, "col", level_bit)
        state = combine(state, partner, own_pattern(level_bit), translations)
    for level_bit in range(local_bits):
        partner = pair_flip(state, level_bit)
        state = combine(state, partner, own_pattern(col_bits + level_bit), translations)
    first_row_level = col_bits + local_bits
    for level_bit in range(row_bits):
        partner = swapped(state, "row", level_bit)
        state = combine(state, partner, own_pattern(first_row_level + level_bit), translations)
    expand = expand_maps.reshape(boxes_here, LEAF, RANK)
    result = jnp.einsum("jlr,jrk->jlk", expand, state, preferred_element_type=jnp.float32).astype(
        jnp.bfloat16
    )
    return result.reshape(boxes_here, LEAF * VECS)


def solution(mesh):
    placed = (P(("col", "row"), None), P(("col", "row"), None), P(("col", "row"), None), P(), P())
    return jax.shard_map(
        local, mesh=mesh, in_specs=placed, out_specs=P(("col", "row"), None), check_vma=False
    )
```

profile of v0, /device:TPU:0, one launch (start us, length us, event | category | flops | bytes accessed | tf_op | source)
XLA Modules:
  0.0 332.2 jit_solution(5613860083272169898)
XLA Ops:
  19.4 5.4 %fusion.190 = (s32[1,16384]{1,0:T(1,128)}, s32[1,16384]{1,0:T(1,128)}, s32[1,16384]{1,0:T(1,128)}, s32[1,16384]{1,0:T(1,128)}, s32[1,16384]{1,0:T(1,128)}, /*ind...) fusion(s32[14,16384]{1,0:T(8,128)} %param.8), kind=kLoop, calls=%fused_computation.199 | loop fusion | bytes 1835008 | tf_op jit(solution)/shard_map/slice | solution.py:47
  28.2 14.7 %collective-permute-done = bf16[128,64,64]{0,2,1:T(8,128)(2,1)} collective-permute-done((bf16[128,64,64]{0,2,1:T(8,128)(2,1)}, bf16[128,64,64]{0,2,1:T(8,128)(2,1)}, u32[]{:S(2)}, u32[]{:S(2)}) %collective-permute-start) | collective-permute-done | bytes 1048608 | tf_op jit(solution)/shard_map/ppermute | solution.py:12
  42.9 5.5 %copy.20 = bf16[128,64,64]{1,2,0:T(8,128)(2,1)} copy(bf16[128,64,64]{0,2,1:T(8,128)(2,1)} %collective-permute-done) | data formatting | bytes 2097152 | tf_op jit(solution)/shard_map/ppermute | solution.py:12
  48.4 4.9 %fusion.102 = bf16[128,64,64]{1,2,0:T(8,128)(2,1)} fusion(bf16[128,64,128]{2,1,0:T(8,128)(2,1)} %bitcast.168, bf16[128,64,64]{1,2,0:T(8,128)(2,1)} %copy.20, bf16[128,64,64]{1,2,0:T(8,128)(2,1)S(1)} %convolution_convert_fusion.14), kind=kOutput, calls=%fused_computation.85 | convolution fusion | flops 138936320 | bytes 5242880 | tf_op jit(solution)/shard_map/brt,btk->brk/dot_general | solution.py:31
  53.3 4.5 %copy.21 = bf16[128,64,64]{0,2,1:T(8,128)(2,1)S(1)} copy(bf16[128,64,64]{1,2,0:T(8,128)(2,1)} %fusion.102) | data formatting | bytes 2097152 | tf_op jit(solution)/shard_map/convert_element_type | solution.py:32
  69.8 13.7 %collective-permute-done.1 = bf16[128,64,64]{0,2,1:T(8,128)(2,1)S(1)} collective-permute-done((bf16[128,64,64]{0,2,1:T(8,128)(2,1)S(1)}, bf16[128,64,64]{0,2,1:T(8,128)(2,1)S(1)}, u32[]{:S(2)}, u32[]{:S(2)}) %collective-permute-start.1) | collective-permute-done | bytes 1048608 | tf_op jit(solution)/shard_map/ppermute | solution.py:12
  121.4 5.9 %copy.24 = bf16[128,64,64]{1,2,0:T(8,128)(2,1)} copy(bf16[128,64,64]{0,2,1:T(8,128)(2,1)} %collective-permute-done.2) | data formatting | bytes 2097152 | tf_op jit(solution)/shard_map/ppermute | solution.py:12
  127.3 4.8 %fusion.96 = bf16[128,64,64]{1,2,0:T(8,128)(2,1)} fusion(bf16[128,64,128]{2,1,0:T(8,128)(2,1)} %bitcast.164, bf16[128,64,64]{1,2,0:T(8,128)(2,1)} %copy.24, bf16[128,64,64]{1,2,0:T(8,128)(2,1)S(1)} %fusion.99), kind=kOutput, calls=%fused_computation.83 | convolution fusion | flops 138936320 | bytes 5242880 | tf_op jit(solution)/shard_map/brt,btk->brk/dot_general | solution.py:31
  135.4 4.9 %fusion.93 = bf16[128,64,64]{1,2,0:T(8,128)(2,1)} fusion(bf16[128,64,128]{2,1,0:T(8,128)(2,1)} %bitcast.161, bf16[128,64,64]{1,2,0:T(8,128)(2,1)} %bitcast.172, bf16[128,64,64]{1,2,0:T(8,128)(2,1)S(1)} %copy-done.2), kind=kOutput, calls=%fused_computation.82 | convolution fusion | flops 138936320 | bytes 5242880 | tf_op jit(solution)/shard_map/brt,btk->brk/dot_general | solution.py:31
  143.6 4.9 %fusion.90 = bf16[128,64,64]{1,2,0:T(8,128)(2,1)} fusion(bf16[128,64,128]{2,1,0:T(8,128)(2,1)} %bitcast.159, bf16[128,64,64]{1,2,0:T(8,128)(2,1)} %bitcast.173, bf16[128,64,64]{1,2,0:T(8,128)(2,1)S(1)} %copy-done.3), kind=kOutput, calls=%fused_computation.81 | convolution fusion | flops 138936320 | bytes 5242880 | tf_op jit(solution)/shard_map/brt,btk->brk/dot_general | solution.py:31
  151.8 4.8 %fusion.87 = bf16[128,64,64]{1,2,0:T(8,128)(2,1)} fusion(bf16[128,64,128]{2,1,0:T(8,128)(2,1)} %bitcast.160, bf16[128,64,64]{1,2,0:T(8,128)(2,1)} %bitcast.174, bf16[128,64,64]{1,2,0:T(8,128)(2,1)S(1)} %copy-done.4), kind=kOutput, calls=%fused_computation.80 | convolution fusion | flops 138936320 | bytes 5242880 | tf_op jit(solution)/shard_map/brt,btk->brk/dot_general | solution.py:31
  160.0 4.9 %fusion.84 = bf16[128,64,64]{1,2,0:T(8,128)(2,1)} fusion(bf16[128,64,128]{2,1,0:T(8,128)(2,1)} %bitcast.162, bf16[128,64,64]{1,2,0:T(8,128)(2,1)} %bitcast.175, bf16[128,64,64]{1,2,0:T(8,128)(2,1)S(1)} %copy-done.5), kind=kOutput, calls=%fused_computation.79 | convolution fusion | flops 138936320 | bytes 5242880 | tf_op jit(solution)/shard_map/brt,btk->brk/dot_general | solution.py:31
  168.2 4.9 %fusion.81 = bf16[128,64,64]{1,2,0:T(8,128)(2,1)} fusion(bf16[128,64,128]{2,1,0:T(8,128)(2,1)} %bitcast.163, bf16[128,64,64]{1,2,0:T(8,128)(2,1)} %bitcast.176, bf16[128,64,64]{1,2,0:T(8,128)(2,1)S(1)} %copy-done.6), kind=kOutput, calls=%fused_computation.78 | convolution fusion | flops 138936320 | bytes 5242880 | tf_op jit(solution)/shard_map/brt,btk->brk/dot_general | solution.py:31
  176.5 4.9 %fusion.78 = bf16[128,64,64]{1,2,0:T(8,128)(2,1)} fusion(bf16[128,64,128]{2,1,0:T(8,128)(2,1)} %bitcast.165, bf16[128,64,64]{1,2,0:T(8,128)(2,1)} %bitcast.177, bf16[128,64,64]{1,2,0:T(8,128)(2,1)S(1)} %copy-done.7), kind=kOutput, calls=%fused_computation.77 | convolution fusion | flops 138936320 | bytes 5242880 | tf_op jit(solution)/shard_map/brt,btk->brk/dot_general | solution.py:31
  195.7 5.5 %copy.26 = bf16[128,64,64]{1,2,0:T(8,128)(2,1)} copy(bf16[128,64,64]{0,2,1:T(8,128)(2,1)} %collective-permute-done.3) | data formatting | bytes 2097152 | tf_op jit(solution)/shard_map/ppermute | solution.py:12
  201.2 4.9 %fusion.72 = bf16[128,64,64]{1,2,0:T(8,128)(2,1)} fusion(bf16[128,64,128]{2,1,0:T(8,128)(2,1)} %bitcast.169, bf16[128,64,64]{1,2,0:T(8,128)(2,1)} %copy.26, bf16[128,64,64]{1,2,0:T(8,128)(2,1)S(1)} %fusion.75), kind=kOutput, calls=%fused_computation.75 | convolution fusion | flops 138936320 | bytes 5242880 | tf_op jit(solution)/shard_map/brt,btk->brk/dot_general | solution.py:31
  206.0 4.5 %copy.27 = bf16[128,64,64]{0,2,1:T(8,128)(2,1)S(1)} copy(bf16[128,64,64]{1,2,0:T(8,128)(2,1)} %fusion.72) | data formatting | bytes 2097152 | tf_op jit(solution)/shard_map/convert_element_type | solution.py:32
  215.4 20.8 %collective-permute-done.4 = bf16[128,64,64]{0,2,1:T(8,128)(2,1)S(1)} collective-permute-done((bf16[128,64,64]{0,2,1:T(8,128)(2,1)S(1)}, bf16[128,64,64]{0,2,1:T(8,128)(2,1)S(1)}, u32[]{:S(2)}, u32[]{:S(2)}) %collective-permute-start.4) | collective-permute-done | bytes 1048608 | tf_op jit(solution)/shard_map/ppermute | solution.py:12
  236.2 4.7 %copy.28 = bf16[128,64,64]{1,2,0:T(8,128)(2,1)} copy(bf16[128,64,64]{0,2,1:T(8,128)(2,1)S(1)} %collective-permute-done.4) | data formatting | bytes 2097152 | tf_op jit(solution)/shard_map/ppermute | solution.py:12
  255.5 20.3 %collective-permute-done.5 = bf16[128,64,64]{0,2,1:T(8,128)(2,1)} collective-permute-done((bf16[128,64,64]{0,2,1:T(8,128)(2,1)}, bf16[128,64,64]{0,2,1:T(8,128)(2,1)}, u32[]{:S(2)}, u32[]{:S(2)}) %collective-permute-start.5) | collective-permute-done | bytes 1048608 | tf_op jit(solution)/shard_map/ppermute | solution.py:12
  275.8 5.5 %copy.30 = bf16[128,64,64]{1,2,0:T(8,128)(2,1)} copy(bf16[128,64,64]{0,2,1:T(8,128)(2,1)} %collective-permute-done.5) | data formatting | bytes 2097152 | tf_op jit(solution)/shard_map/ppermute | solution.py:12
  299.3 14.2 %collective-permute-done.6 = bf16[128,64,64]{0,2,1:T(8,128)(2,1)} collective-permute-done((bf16[128,64,64]{0,2,1:T(8,128)(2,1)}, bf16[128,64,64]{0,2,1:T(8,128)(2,1)}, u32[]{:S(2)}, u32[]{:S(2)}) %collective-permute-start.6) | collective-permute-done | bytes 1048608 | tf_op jit(solution)/shard_map/ppermute | solution.py:12
  313.6 5.5 %copy.32 = bf16[128,64,64]{1,2,0:T(8,128)(2,1)} copy(bf16[128,64,64]{0,2,1:T(8,128)(2,1)} %collective-permute-done.6) | data formatting | bytes 2097152 | tf_op jit(solution)/shard_map/ppermute | solution.py:12
  319.1 7.0 %convert_bitcast_fusion = bf16[128,64,64]{1,2,0:T(8,128)(2,1)} fusion(bf16[128,64,64]{2,1,0:T(8,128)(2,1)} %copy.35, bf16[128,64,128]{2,1,0:T(8,128)(2,1)} %bitcast.158, bf16[128,64,64]{1,2,0:T(8,128)(2,1)} %copy.32, bf16[128,64,64]{1,2,0:T(8,128)(2,1)S(1)} %fusion.66), kind=kOutput, calls=%fused_computation.70 | convolution fusion | flops 206569472 | bytes 6291456 | tf_op jit(solution)/shard_map/jlr,jrk->jlk/dot_general | solution.py:65
  (92 shorter events, 149.9 us)
Async XLA Ops:
  1.6 3.7 %copy-start.10 = (bf16[128,4096]{1,0:T(8,128)(2,1)S(1)}, bf16[128,4096]{1,0:T(8,128)(2,1)}, u32[]{:S(2)}) copy-start(bf16[128,4096]{1,0:T(8,128)(2,1)} %param.5) | copy-start | bytes 3145732
  13.4 12.0 %copy-start = (bf16[64,64,128]{2,1,0:T(8,128)(2,1)S(1)}, bf16[64,64,128]{2,1,0:T(8,128)(2,1)}, u32[]{:S(2)}) copy-start(bf16[64,64,128]{2,1,0:T(8,128)(2,1)} %param.9) | copy-start | bytes 3145732
  17.3 25.6 %collective-permute-start = (bf16[128,64,64]{0,2,1:T(8,128)(2,1)}, bf16[128,64,64]{0,2,1:T(8,128)(2,1)}, u32[]{:S(2)}, u32[]{:S(2)}) collective-permute-start(bf16[128,64,64]{0,2,1:T(8,128)(2,1)} %copy.19), channel_id=1, source_target_pairs={{0,16},{16,0},{32,48},{48,32},{64,80},{80,64},{96,112},{112,96},{1... | collective-permute-start | bytes 3145736 | tf_op jit(solution)/shard_map/ppermute | solution.py:12
  57.8 25.8 %collective-permute-start.1 = (bf16[128,64,64]{0,2,1:T(8,128)(2,1)S(1)}, bf16[128,64,64]{0,2,1:T(8,128)(2,1)S(1)}, u32[]{:S(2)}, u32[]{:S(2)}) collective-permute-start(bf16[128,64,64]{0,2,1:T(8,128)(2,1)S(1)} %copy.21), channel_id=1, source_target_pairs={{0,32},{16,48},{32,0},{48,16},{64,96},{80,112},{96,64},{112,80},{1... | collective-permute-start | bytes 3145736 | tf_op jit(solution)/shard_map/ppermute | solution.py:12
  96.1 4.5 %copy-start.8 = (bf16[16,8,64,128]{3,1,2,0:T(8,128)(2,1)S(1)}, bf16[16,8,64,128]{3,1,2,0:T(8,128)(2,1)}, u32[]{:S(2)}) copy-start(bf16[16,8,64,128]{3,1,2,0:T(8,128)(2,1)} %fusion.116) | copy-start | bytes 6291460
  96.1 25.3 %collective-permute-start.2 = (bf16[128,64,64]{0,2,1:T(8,128)(2,1)}, bf16[128,64,64]{0,2,1:T(8,128)(2,1)}, u32[]{:S(2)}, u32[]{:S(2)}) collective-permute-start(bf16[128,64,64]{0,2,1:T(8,128)(2,1)} %copy.23), channel_id=1, source_target_pairs={{0,64},{16,80},{32,96},{48,112},{64,0},{80,16},{96,32},{112,48},{1... | collective-permute-start | bytes 3145736 | tf_op jit(solution)/shard_map/ppermute | solution.py:12
  100.6 1.9 copy-start.9
  132.1 3.2 copy-start.2
  140.2 3.4 %copy-start.3 = (bf16[128,64,64]{1,2,0:T(8,128)(2,1)S(1)}, bf16[128,64,64]{1,2,0:T(8,128)(2,1)}, u32[]{:S(2)}) copy-start(bf16[128,64,64]{1,2,0:T(8,128)(2,1)} %fusion.93) | copy-start | bytes 3145732
  148.4 3.4 %copy-start.4 = (bf16[128,64,64]{1,2,0:T(8,128)(2,1)S(1)}, bf16[128,64,64]{1,2,0:T(8,128)(2,1)}, u32[]{:S(2)}) copy-start(bf16[128,64,64]{1,2,0:T(8,128)(2,1)} %fusion.90) | copy-start | bytes 3145732
  156.7 3.4 %copy-start.5 = (bf16[128,64,64]{1,2,0:T(8,128)(2,1)S(1)}, bf16[128,64,64]{1,2,0:T(8,128)(2,1)}, u32[]{:S(2)}) copy-start(bf16[128,64,64]{1,2,0:T(8,128)(2,1)} %fusion.87) | copy-start | bytes 3145732
  164.9 3.3 copy-start.6
  173.2 3.3 copy-start.7
  192.7 3.0 collective-permute-start.3
  210.5 25.6 %collective-permute-start.4 = (bf16[128,64,64]{0,2,1:T(8,128)(2,1)S(1)}, bf16[128,64,64]{0,2,1:T(8,128)(2,1)S(1)}, u32[]{:S(2)}, u32[]{:S(2)}) collective-permute-start(bf16[128,64,64]{0,2,1:T(8,128)(2,1)S(1)} %copy.27), channel_id=1, source_target_pairs={{0,2},{1,3},{2,0},{3,1},{4,6},{5,7},{6,4},{7,5},{8,10},{9,11},{10,... | collective-permute-start | bytes 3145736 | tf_op jit(solution)/shard_map/ppermute | solution.py:12
  245.1 8.5 %copy-start.1 = (bf16[128,64,64]{1,2,0:T(8,128)(2,1)}, bf16[128,64,64]{1,2,0:T(8,128)(2,1)S(1)}, u32[]{:S(2)}) copy-start(bf16[128,64,64]{1,2,0:T(8,128)(2,1)S(1)} %fusion.69) | copy-start | bytes 3145732
  249.0 26.8 %collective-permute-start.5 = (bf16[128,64,64]{0,2,1:T(8,128)(2,1)}, bf16[128,64,64]{0,2,1:T(8,128)(2,1)}, u32[]{:S(2)}, u32[]{:S(2)}) collective-permute-start(bf16[128,64,64]{0,2,1:T(8,128)(2,1)} %copy.29), channel_id=1, source_target_pairs={{0,4},{1,5},{2,6},{3,7},{4,0},{5,1},{6,2},{7,3},{8,12},{9,13},{10,... | collective-permute-start | bytes 3145736 | tf_op jit(solution)/shard_map/ppermute | solution.py:12
  289.3 24.2 %collective-permute-start.6 = (bf16[128,64,64]{0,2,1:T(8,128)(2,1)}, bf16[128,64,64]{0,2,1:T(8,128)(2,1)}, u32[]{:S(2)}, u32[]{:S(2)}) collective-permute-start(bf16[128,64,64]{0,2,1:T(8,128)(2,1)} %copy.31), channel_id=1, source_target_pairs={{0,8},{1,9},{2,10},{3,11},{4,12},{5,13},{6,14},{7,15},{8,0},{9,1},... | collective-permute-start | bytes 3145736 | tf_op jit(solution)/shard_map/ppermute | solution.py:12
where the time goes:
time: 337 us; the launch traced here: 332 us
  local copies, waits for them, and re-layouts  146 us (43%)
  matrix products  85.1 us (25%)
  waiting for transfers between devices  84.4 us (25%)
  starting transfers between devices  16.5 us (5%)
    ppermute x7, waiting for transfers between devices, swapped(): lax.ppermute(array, axis, [(i, i ^ 1 << stride) for i in range(lax.axis_s...  84.4 us
    dot_general x13, matrix products, combine(): jnp.einsum('brt,btk->brk', mats, stacked, preferred_element_type=jnp.floa...  60.5 us
    ppermute x7, local copies, waits for them, and re-layouts, swapped(): lax.ppermute(array, axis, [(i, i ^ 1 << stride) for i in range(lax.axis_s...  37 us
    unnamed x39, local copies, waits for them, and re-layouts  31.1 us
    convert_element_type x6, local copies, waits for them, and re-layouts, combine(): return summed.astype(jnp.bfloat16)  24.8 us
    rev x7, local copies, waits for them, and re-layouts, pair_flip(): return jnp.flip(shaped, 1).reshape(values.shape)  23 us
    ppermute x7, starting transfers between devices, swapped(): lax.ppermute(array, axis, [(i, i ^ 1 << stride) for i in range(lax.axis_s...  16.5 us
    dot_general x14, matrix products, combine(): jnp.dot(selector, table, preferred_element_type=jnp.float32)  14.7 us
  transfers between devices with their start and end apart: 7, of which 7 were waited for; matrix products, arithmetic and copies ran while one was open for 17% of the time, Pallas kernels for 0%

commit v1 on v0

v1 whole, which is shorter than its diff:
```python
import functools

import jax
import jax.numpy as jnp
from jax import lax
from jax.experimental import pallas as pl
from jax.experimental.pallas import tpu as pltpu
from jax.sharding import Mesh, PartitionSpec as P

LEAF = 64
RANK = 64
VECS = 64
WIDE = 2 * VECS
TILES = 64
AXES = ("yh", "x", "yl", "z", "core")
CHIPS = ("yh", "x", "yl", "z")


def left_half(shape):
    return lax.broadcasted_iota(jnp.int32, shape, len(shape) - 1) < VECS


def halves(tile):
    left = left_half(tile.shape)
    zero = jnp.zeros_like(tile)
    return jnp.where(left, tile, zero), jnp.where(left, zero, tile)


def swap_halves(tile):
    return jnp.concatenate([tile[:, VECS:], tile[:, :VECS]], axis=1)


def dot(lhs, rhs):
    return jnp.dot(lhs, rhs, preferred_element_type=jnp.float32).astype(jnp.bfloat16)


def tile_level(src, dst, near, swapped, chosen, bit, place=lambda tile: tile, unroll=4):
    def step(pair, carry):
        a = ((pair >> bit) << (bit + 1)) | (pair & ((1 << bit) - 1))
        b = a + (1 << bit)
        al, ar = halves(src[a])
        bl, br = halves(src[b])
        weights = jnp.concatenate([al, bl, ar, br], axis=0)
        for_a = jnp.concatenate([near[chosen(a, 0)], near[chosen(a, 1)]], axis=1)
        for_b = jnp.concatenate([swapped[chosen(b, 0)], swapped[chosen(b, 1)]], axis=1)
        out = dot(jnp.concatenate([for_a, for_b], axis=0), weights)
        dst[place(a)] = out[:RANK]
        dst[place(b)] = out[RANK:]
        return carry

    lax.fori_loop(0, TILES // 2, step, 0, unroll=unroll)


def lane_level(src, dst, near, chosen, unroll=4):
    def step(a, carry):
        tile = src[a]
        al, ar = halves(tile)
        bl, br = halves(swap_halves(tile))
        weights = jnp.concatenate([al, bl, ar, br], axis=0)
        for_a = jnp.concatenate([near[chosen(a, 0)], near[chosen(a, 1)]], axis=1)
        dst[a] = dot(for_a, weights)
        return carry

    lax.fori_loop(0, TILES, step, 0, unroll=unroll)


def other_level(src, partner, dst, near, chosen, unroll=4):
    def step(a, carry):
        al, ar = halves(src[a])
        bl, br = halves(partner[a])
        weights = jnp.concatenate([al, bl, ar, br], axis=0)
        for_a = jnp.concatenate([near[chosen(a, 0)], near[chosen(a, 1)]], axis=1)
        dst[a] = dot(for_a, weights)
        return carry

    lax.fori_loop(0, TILES, step, 0, unroll=unroll)


def leaf_kernel(maps, vectors, out):
    def step(group, carry):
        tile = group * 2
        box = (tile >> 3) * 16 + (tile & 7)
        order = (box, box + 8, box + 1, box + 9)
        v = jnp.concatenate([maps[j] for j in order], axis=0).T
        lhs = jnp.concatenate([v[:RANK], v[RANK:]], axis=1)
        zero = jnp.zeros((LEAF // 2, WIDE), jnp.bfloat16)
        even, odd = [], []
        for place, j in enumerate(order):
            raw = vectors[j]
            el, orr = halves(raw)
            turned = swap_halves(raw)
            ol, er = halves(turned)
            e, o = (el, ol) if place % 2 == 0 else (er, orr)
            even.append([e, zero] if place < 2 else [zero, e])
            odd.append([o, zero] if place < 2 else [zero, o])
        weights = jnp.concatenate([jnp.concatenate(r, axis=1) for r in even + odd], axis=0)
        both = dot(lhs, weights)
        out[tile] = both[:, :WIDE]
        out[tile + 1] = both[:, WIDE:]
        return carry

    lax.fori_loop(0, TILES // 2, step, 0, unroll=2)


def first_kernel(chosen_ref, state, near, swapped, out, one, two):
    def chosen(level):
        return lambda tile, half: chosen_ref[level * 128 + (tile >> 3) * 16 + half * 8 + (tile & 7)]

    bufs = [state, one, two, one, two, one, two]
    for level, bit in enumerate((3, 4, 5, 0, 1, 2)):
        tile_level(bufs[level], bufs[level + 1], near, swapped, chosen(level), bit)
    lane_level(two, out, near, chosen(6))


def second(chosen_ref, level):
    return lambda tile, half: chosen_ref[level * 128 + (tile & 7) * 16 + (tile >> 3) * 2 + half]


def second_kernel(chosen_ref, state, near, swapped, out, one, two):
    bufs = [state, one, two, out]
    for level, bit in enumerate((3, 4, 5)):
        tile_level(bufs[level], bufs[level + 1], near, swapped, second(chosen_ref, level), bit)


def third_kernel(chosen_ref, state, partner, near, swapped, out, one, two):
    other_level(state, partner, one, near, second(chosen_ref, 3))
    tile_level(one, two, near, swapped, second(chosen_ref, 4), 0)
    tile_level(two, one, near, swapped, second(chosen_ref, 5), 1)
    turn = lambda tile: (tile & 7) * 8 + (tile >> 3)
    tile_level(one, out, near, swapped, second(chosen_ref, 6), 2, place=turn)


def expand_kernel(state, maps, out):
    def step(tile, carry):
        box = (tile & 7) * 16 + (tile >> 3)
        both = state[tile]
        al, ar = halves(both)
        bl, br = halves(swap_halves(both))
        out[box] = dot(maps[box], jnp.concatenate([al, br], axis=0))
        out[box + 8] = dot(maps[box + 8], jnp.concatenate([bl, ar], axis=0))
        return carry

    lax.fori_loop(0, TILES, step, 0, unroll=4)


VM = pl.BlockSpec(memory_space=pltpu.VMEM)
SM = pl.BlockSpec(memory_space=pltpu.SMEM)
PARAMS = pltpu.CompilerParams(vmem_limit_bytes=32 * 1024 * 1024)
STATE = jax.ShapeDtypeStruct((TILES, RANK, WIDE), jnp.bfloat16)


def local(inputs, leaf_maps, expand_maps, patterns, translations):
    boxes = inputs.shape[0]
    col_place = lax.axis_index("yh") * 4 + lax.axis_index("x")
    row_low = lax.axis_index("yl") * 4 + lax.axis_index("z")
    core = lax.axis_index("core")
    scratch = [pltpu.VMEM(STATE.shape, STATE.dtype)] * 2

    swapped = jnp.concatenate([translations[:, :, RANK:], translations[:, :, :RANK]], axis=2)
    row = row_low * 2 + core
    first_chosen = lax.dynamic_slice(
        patterns[:7].reshape(7, 8, 2048), (0, 0, row * 128 + col_place * 16), (7, 8, 16)
    ).reshape(-1)
    second_chosen = lax.dynamic_slice(patterns, (7, col_place * 2048), (7, 2048))
    second_chosen = lax.dynamic_slice(
        second_chosen.reshape(7, 8, 2, 16, 8), (0, 0, core, 0, row_low), (7, 8, 1, 16, 1)
    ).reshape(-1)

    shaped = (boxes, LEAF // 2, WIDE)
    state = pl.pallas_call(
        leaf_kernel, out_shape=STATE, in_specs=[VM, VM], out_specs=VM, compiler_params=PARAMS
    )(leaf_maps.reshape(shaped), inputs.reshape(shaped))
    state = lax.all_to_all(state, ("yh", "x"), 0, 0, tiled=True)
    state = pl.pallas_call(
        first_kernel, out_shape=STATE, in_specs=[SM, VM, VM, VM], out_specs=VM,
        scratch_shapes=scratch, compiler_params=PARAMS,
    )(first_chosen, state, translations, swapped)
    state = lax.all_to_all(state, CHIPS, 0, 0, tiled=True)
    state = pl.pallas_call(
        second_kernel, out_shape=STATE, in_specs=[SM, VM, VM, VM], out_specs=VM,
        scratch_shapes=scratch, compiler_params=PARAMS,
    )(second_chosen, state, translations, swapped)
    partner = lax.ppermute(state, "core", [(0, 1), (1, 0)])
    state = pl.pallas_call(
        third_kernel, out_shape=STATE, in_specs=[SM, VM, VM, VM, VM], out_specs=VM,
        scratch_shapes=scratch, compiler_params=PARAMS,
    )(second_chosen, state, partner, translations, swapped)
    state = lax.all_to_all(state, ("yl", "z"), 0, 0, tiled=True)
    result = pl.pallas_call(
        expand_kernel, out_shape=jax.ShapeDtypeStruct(shaped, jnp.bfloat16),
        in_specs=[VM, VM], out_specs=VM, compiler_params=PARAMS,
    )(state, expand_maps.reshape(shaped))
    return result.reshape(boxes, LEAF * VECS)


def solution(mesh):
    fine = Mesh(mesh.devices.reshape(2, 4, 2, 4, 2), AXES)
    rows = P(AXES, None)
    return jax.shard_map(
        local, mesh=fine, in_specs=(rows, rows, rows, P(), P()), out_specs=rows, check_vma=False
    )
```

time: 337 us -> 116 us (0.34); the launches traced: 332 us -> 115 us
  local copies, waits for them, and re-layouts: 146 us -> 12 us
  matrix products: 85.1 us -> 0 us
  waiting for transfers between devices: 84.4 us -> 45.8 us
  Pallas kernels: 0 us -> 38.4 us
    dot_general x29 -> x0, matrix products: 85.1 us -> none  [the longest x13 60.5 us: combine(): jnp.einsum('brt,btk->brk', mats, stacked, preferred_element_type=jnp.floa...]
    ppermute x7 -> x1, waiting for transfers between devices: 84.4 us -> 2.65 us  [local(): partner = lax.ppermute(state, 'core', [(0, 1), (1, 0)])]
    all_to_all x0 -> x3, waiting for transfers between devices: none -> 43.2 us  [the longest x1 15 us: local(): state = lax.all_to_all(state, ('yl', 'z'), 0, 0, tiled=True)]
    pallas_call x0 -> x5, Pallas kernels: none -> 38.4 us  [the longest x1 14.9 us: local(): pl.pallas_call(first_kernel, out_shape=STATE, in_specs=[SM, VM, VM, VM],...]
    ppermute x7 -> x0, local copies, waits for them, and re-layouts: 37 us -> none  [swapped(): lax.ppermute(array, axis, [(i, i ^ 1 << stride) for i in range(lax.axis_s...]
    convert_element_type x8 -> x0, local copies, waits for them, and re-layouts: 33.2 us -> none  [the longest x6 24.8 us: combine(): return summed.astype(jnp.bfloat16)]
    unnamed x39 -> x15, local copies, waits for them, and re-layouts: 31.1 us -> 5.65 us
    rev x7 -> x0, local copies, waits for them, and re-layouts: 23 us -> none  [pair_flip(): return jnp.flip(shaped, 1).reshape(values.shape)]
  transfers between devices with their start and end apart: 7 -> 4, of which waited for: 7 -> 4; matrix products, arithmetic and copies ran while one was open for 17% -> 6% of each run, Pallas kernels for 0% -> 0%
where the time goes in v1:
time: 116 us; the launch traced here: 115 us
  waiting for transfers between devices  45.8 us (39%)
  Pallas kernels  38.4 us (33%)
  starting transfers between devices  18 us (16%)
  local copies, waits for them, and re-layouts  12 us (10%)
    all_to_all x1, waiting for transfers between devices, local(): state = lax.all_to_all(state, ('yl', 'z'), 0, 0, tiled=True)  15 us
    pallas_call x1, Pallas kernels, local(): pl.pallas_call(first_kernel, out_shape=STATE, in_specs=[SM, VM, VM, VM],...  14.9 us
    all_to_all x1, waiting for transfers between devices, local(): state = lax.all_to_all(state, ('yh', 'x'), 0, 0, tiled=True)  14.6 us
    all_to_all x1, waiting for transfers between devices, local(): state = lax.all_to_all(state, CHIPS, 0, 0, tiled=True)  13.5 us
    pallas_call x1, Pallas kernels, local(): pl.pallas_call(third_kernel, out_shape=STATE, in_specs=[SM, VM, VM, VM, V...  8.72 us
    all_to_all x1, starting transfers between devices, local(): state = lax.all_to_all(state, CHIPS, 0, 0, tiled=True)  7.22 us
    all_to_all x1, starting transfers between devices, local(): state = lax.all_to_all(state, ('yh', 'x'), 0, 0, tiled=True)  7.02 us
    pallas_call x1, Pallas kernels, local(): pl.pallas_call(second_kernel, out_shape=STATE, in_specs=[SM, VM, VM, VM],...  5.88 us
  transfers between devices with their start and end apart: 4, of which 4 were waited for; matrix products, arithmetic and copies ran while one was open for 6% of the time, Pallas kernels for 0%

profile of v1, /device:TPU:0, one launch (start us, length us, event | category | flops | bytes accessed | tf_op | source)
XLA Modules:
  0.0 115.1 jit_solution(13970885538279353995)
XLA Ops:
  0.0 1.5 %copy.7 = bf16[16,8,32,128]{3,2,1,0:T(8,128)(2,1)S(1)} copy(bf16[16,8,32,128]{3,1,2,0:T(8,128)(2,1)} %bitcast.19) | data formatting | bytes 2097152
  1.8 4.9 %shard_map.55 = bf16[64,64,128]{2,1,0:T(8,128)(2,1)} custom-call(bf16[128,32,128]{2,1,0:T(8,128)(2,1)S(1)} %bitcast.16, bf16[128,32,128]{2,1,0:T(8,128)(2,1)S(1)} %bitcast.17), custom_call_target="tpu_custom_call" | custom-call | tf_op jit(solution)/shard_map/pallas_call | solution.py:170
  6.7 7.0 %all-to-all-start = ((bf16[64,64,128]{2,1,0:T(8,128)(2,1)}), bf16[64,64,128]{2,1,0:T(8,128)(2,1)S(1)}, u32[]{:S(2)}, u32[]{:S(2)}) async-start(bf16[64,64,128]{2,1,0:T(8,128)(2,1)} %shard_map.55), calls=%async_computation | async-start | bytes 2097152 | tf_op jit(solution)/shard_map/all_to_all | solution.py:173
  13.7 1.0 slice-done
  14.7 0.3 copy.14
  15.2 0.5 fusion
  15.7 0.6 pad_maximum_fusion.swapped
  16.3 14.6 %all-to-all-done.state = bf16[64,64,128]{2,1,0:T(8,128)(2,1)S(1)} async-done(((bf16[64,64,128]{2,1,0:T(8,128)(2,1)}), bf16[64,64,128]{2,1,0:T(8,128)(2,1)S(1)}, u32[]{:S(2)}, u32[]{:S(2)}) %all-to-all-start) | async-done | bytes 1048608 | tf_op jit(solution)/shard_map/all_to_all | solution.py:173
  30.9 14.9 %shard_map.56 = bf16[64,64,128]{2,1,0:T(8,128)(2,1)S(1)} custom-call(s32[896]{0:T(1024)S(1)} %reshape.27.chosen_ref, bf16[64,64,128]{2,1,0:T(8,128)(2,1)S(1)} %all-to-all-done.state, bf16[64,64,128]{2,1,0:T(8,128)(2,1)S(1)} %copy-done, bf16[64,64,128]{2,1,0:T(8,128)(2,1)S(1)} %pad_maximum_fusion.swapped), custom_call_target="tpu_custom_call" | custom-call | tf_op jit(solution)/shard_map/pallas_call | solution.py:174
  45.8 1.0 copy-done.1
  46.8 7.2 %all-to-all-start.1 = ((bf16[64,64,128]{2,1,0:T(8,128)(2,1)}), bf16[64,64,128]{2,1,0:T(8,128)(2,1)S(1)}, u32[]{:S(2)}, u32[]{:S(2)}) async-start(bf16[64,64,128]{2,1,0:T(8,128)(2,1)} %copy-done.1), calls=%async_computation.1 | async-start | bytes 2097152 | tf_op jit(solution)/shard_map/all_to_all | solution.py:178
  54.0 1.0 constant_dynamic-slice_fusion.1
  55.0 1.4 %reshape.24 = s32[7,8,2,16,8]{4,3,2,1,0:T(8,128)} reshape(s32[7,2048]{1,0:T(8,128)S(1)} %constant_dynamic-slice_fusion.1) | data formatting | bytes 114688 | tf_op jit(solution)/shard_map/reshape | solution.py:166
  56.5 2.2 %dynamic-slice_reduce_fusion = s32[7,8,16]{2,1,0:T(8,128)S(1)} fusion(s32[7,8,2,16,8]{4,3,2,1,0:T(8,128)} %reshape.24, s32[]{:T(128)S(6)} %select_n.13, s32[]{:T(128)S(6)} %select_n.14), kind=kLoop, calls=%fused_computation.3 | loop fusion | bytes 7176 | tf_op jit(solution)/shard_map/dynamic_slice | solution.py:165
  58.7 13.5 %all-to-all-done.1.state = bf16[64,64,128]{2,1,0:T(8,128)(2,1)S(1)} async-done(((bf16[64,64,128]{2,1,0:T(8,128)(2,1)}), bf16[64,64,128]{2,1,0:T(8,128)(2,1)S(1)}, u32[]{:S(2)}, u32[]{:S(2)}) %all-to-all-start.1) | async-done | bytes 1048608 | tf_op jit(solution)/shard_map/all_to_all | solution.py:178
  72.3 5.9 %shard_map.57.state = bf16[64,64,128]{2,1,0:T(8,128)(2,1)S(1)} custom-call(s32[896]{0:T(1024)S(1)} %reshape.25.chosen_ref, bf16[64,64,128]{2,1,0:T(8,128)(2,1)S(1)} %all-to-all-done.1.state, bf16[64,64,128]{2,1,0:T(8,128)(2,1)S(1)} %copy-done, bf16[64,64,128]{2,1,0:T(8,128)(2,1)S(1)} %pad_maximum_fusion.swapped), custom_call_target="tpu_custom_call" | custom-call | tf_op jit(solution)/shard_map/pallas_call | solution.py:179
  78.2 2.6 %collective-permute-done.partner = bf16[64,64,128]{2,1,0:T(8,128)(2,1)S(1)} collective-permute-done((bf16[64,64,128]{2,1,0:T(8,128)(2,1)S(1)}, bf16[64,64,128]{2,1,0:T(8,128)(2,1)S(1)}, u32[]{:S(2)}, u32[]{:S(2)}) %collective-permute-start) | collective-permute-done | bytes 1048608 | tf_op jit(solution)/shard_map/ppermute | solution.py:183
  80.9 8.7 %shard_map.58 = bf16[64,64,128]{2,1,0:T(8,128)(2,1)S(1)} custom-call(s32[896]{0:T(1024)S(1)} %reshape.25.chosen_ref, bf16[64,64,128]{2,1,0:T(8,128)(2,1)S(1)} %shard_map.57.state, bf16[64,64,128]{2,1,0:T(8,128)(2,1)S(1)} %collective-permute-done.partner, bf16[64,64,128]{2,1,0:T(8,128)(2,1)S(1)} %copy-done, bf16[64,64,128]{2,1,0:T(8,128)(2,1)S(1)} %pad_maximum_fusion.swapped), custom_call_target="tpu_custom_call" | custom-call | tf_op jit(solution)/shard_map/pallas_call | solution.py:184
  89.6 1.0 copy-done.2
  90.6 3.7 %all-to-all-start.2 = ((bf16[64,64,128]{2,1,0:T(8,128)(2,1)}), bf16[64,64,128]{2,1,0:T(8,128)(2,1)S(1)}, u32[]{:S(2)}, u32[]{:S(2)}) async-start(bf16[64,64,128]{2,1,0:T(8,128)(2,1)} %copy-done.2), calls=%async_computation.2 | async-start | bytes 2097152 | tf_op jit(solution)/shard_map/all_to_all | solution.py:188
  94.3 0.2 copy.9
  94.6 15.0 %all-to-all-done.2.state = bf16[64,64,128]{2,1,0:T(8,128)(2,1)S(1)} async-done(((bf16[64,64,128]{2,1,0:T(8,128)(2,1)}), bf16[64,64,128]{2,1,0:T(8,128)(2,1)S(1)}, u32[]{:S(2)}, u32[]{:S(2)}) %all-to-all-start.2) | async-done | bytes 1048608 | tf_op jit(solution)/shard_map/all_to_all | solution.py:188
  109.6 4.0 %shard_map.59 = bf16[128,32,128]{2,1,0:T(8,128)(2,1)S(1)} custom-call(bf16[64,64,128]{2,1,0:T(8,128)(2,1)S(1)} %all-to-all-done.2.state, bf16[128,32,128]{2,1,0:T(8,128)(2,1)S(1)} %bitcast.14), custom_call_target="tpu_custom_call" | custom-call | tf_op jit(solution)/shard_map/pallas_call | solution.py:189
  113.6 1.4 %copy.13 = bf16[16,8,32,128]{3,1,2,0:T(8,128)(2,1)} copy(bf16[16,8,32,128]{3,2,1,0:T(8,128)(2,1)S(1)} %bitcast.15) | data formatting | bytes 2097152
  (14 shorter events, 0.6 us)
Async XLA Ops:
  0.0 1.5 %copy-start.3 = (bf16[128,4096]{1,0:T(8,128)(2,1)S(1)}, bf16[128,4096]{1,0:T(8,128)(2,1)}, u32[]{:S(2)}) copy-start(bf16[128,4096]{1,0:T(8,128)(2,1)} %param.5) | copy-start | bytes 3145732
  6.7 24.2 %all-to-all-start = ((bf16[64,64,128]{2,1,0:T(8,128)(2,1)}), bf16[64,64,128]{2,1,0:T(8,128)(2,1)S(1)}, u32[]{:S(2)}, u32[]{:S(2)}) async-start(bf16[64,64,128]{2,1,0:T(8,128)(2,1)} %shard_map.55), calls=%async_computation | async-start | bytes 2097152 | tf_op jit(solution)/shard_map/all_to_all | solution.py:173
  13.7 1.0 slice-start
  13.7 1.5 %copy-start = (bf16[64,64,128]{2,1,0:T(8,128)(2,1)S(1)}, bf16[64,64,128]{2,1,0:T(8,128)(2,1)}, u32[]{:S(2)}) copy-start(bf16[64,64,128]{2,1,0:T(8,128)(2,1)} %near.5) | copy-start | bytes 3145732
  45.8 1.0 copy-start.1
  46.8 25.5 %all-to-all-start.1 = ((bf16[64,64,128]{2,1,0:T(8,128)(2,1)}), bf16[64,64,128]{2,1,0:T(8,128)(2,1)S(1)}, u32[]{:S(2)}, u32[]{:S(2)}) async-start(bf16[64,64,128]{2,1,0:T(8,128)(2,1)} %copy-done.1), calls=%async_computation.1 | async-start | bytes 2097152 | tf_op jit(solution)/shard_map/all_to_all | solution.py:178
  78.2 2.7 %collective-permute-start = (bf16[64,64,128]{2,1,0:T(8,128)(2,1)S(1)}, bf16[64,64,128]{2,1,0:T(8,128)(2,1)S(1)}, u32[]{:S(2)}, u32[]{:S(2)}) collective-permute-start(bf16[64,64,128]{2,1,0:T(8,128)(2,1)S(1)} %shard_map.57.state), channel_id=1, source_target_pairs={{0,1},{1,0},{2,3},{3,2},{4,5},{5,4},{6,7},{7,6},{8,9},{9,8},{10,11... | collective-permute-start | bytes 3145736 | tf_op jit(solution)/shard_map/ppermute | solution.py:183
  89.6 1.0 copy-start.2
  90.6 3.7 %copy-start.4 = (bf16[128,4096]{1,0:T(8,128)(2,1)S(1)}, bf16[128,4096]{1,0:T(8,128)(2,1)}, u32[]{:S(2)}) copy-start(bf16[128,4096]{1,0:T(8,128)(2,1)} %param.7) | copy-start | bytes 3145732
  90.6 19.0 %all-to-all-start.2 = ((bf16[64,64,128]{2,1,0:T(8,128)(2,1)}), bf16[64,64,128]{2,1,0:T(8,128)(2,1)S(1)}, u32[]{:S(2)}, u32[]{:S(2)}) async-start(bf16[64,64,128]{2,1,0:T(8,128)(2,1)} %copy-done.2), calls=%async_computation.2 | async-start | bytes 2097152 | tf_op jit(solution)/shard_map/all_to_all | solution.py:188

commit v2 on v1

--- a/solution.py
+++ b/solution.py
@@ -1,5 +1,3 @@
-import functools
-
 import jax
 import jax.numpy as jnp
 from jax import lax
@@ -34,8 +32,8 @@
     return jnp.dot(lhs, rhs, preferred_element_type=jnp.float32).astype(jnp.bfloat16)
 
 
-def tile_level(src, dst, near, swapped, chosen, bit, place=lambda tile: tile, unroll=4):
-    def step(pair, carry):
+def tile_level(src, dst, near, swapped, chosen, bit, place=lambda tile: tile):
+    for pair in range(TILES // 2):
         a = ((pair >> bit) << (bit + 1)) | (pair & ((1 << bit) - 1))
         b = a + (1 << bit)
         al, ar = halves(src[a])
@@ -46,38 +44,29 @@
         out = dot(jnp.concatenate([for_a, for_b], axis=0), weights)
         dst[place(a)] = out[:RANK]
         dst[place(b)] = out[RANK:]
-        return carry
-
-    lax.fori_loop(0, TILES // 2, step, 0, unroll=unroll)
 
 
-def lane_level(src, dst, near, chosen, unroll=4):
-    def step(a, carry):
+def lane_level(src, dst, near, chosen):
+    for a in range(TILES):
         tile = src[a]
         al, ar = halves(tile)
         bl, br = halves(swap_halves(tile))
         weights = jnp.concatenate([al, bl, ar, br], axis=0)
         for_a = jnp.concatenate([near[chosen(a, 0)], near[chosen(a, 1)]], axis=1)
         dst[a] = dot(for_a, weights)
-        return carry
-
-    lax.fori_loop(0, TILES, step, 0, unroll=unroll)
 
 
-def other_level(src, partner, dst, near, chosen, unroll=4):
-    def step(a, carry):
+def other_level(src, partner, dst, near, chosen):
+    for a in range(TILES):
         al, ar = halves(src[a])
         bl, br = halves(partner[a])
         weights = jnp.concatenate([al, bl, ar, br], axis=0)
         for_a = jnp.concatenate([near[chosen(a, 0)], near[chosen(a, 1)]], axis=1)
         dst[a] = dot(for_a, weights)
-        return carry
-
-    lax.fori_loop(0, TILES, step, 0, unroll=unroll)
 
 
 def leaf_kernel(maps, vectors, out):
-    def step(group, carry):
+    for group in range(TILES // 2):
         tile = group * 2
         box = (tile >> 3) * 16 + (tile & 7)
         order = (box, box + 8, box + 1, box + 9)
@@ -97,9 +86,6 @@
         both = dot(lhs, weights)
         out[tile] = both[:, :WIDE]
         out[tile + 1] = both[:, WIDE:]
-        return carry
-
-    lax.fori_loop(0, TILES // 2, step, 0, unroll=2)
 
 
 def first_kernel(chosen_ref, state, near, swapped, out, one, two):
@@ -131,16 +117,13 @@
 
 
 def expand_kernel(state, maps, out):
-    def step(tile, carry):
+    for tile in range(TILES):
         box = (tile & 7) * 16 + (tile >> 3)
         both = state[tile]
         al, ar = halves(both)
         bl, br = halves(swap_halves(both))
         out[box] = dot(maps[box], jnp.concatenate([al, br], axis=0))
         out[box + 8] = dot(maps[box + 8], jnp.concatenate([bl, ar], axis=0))
-        return carry
-
-    lax.fori_loop(0, TILES, step, 0, unroll=4)
 
 
 VM = pl.BlockSpec(memory_space=pltpu.VMEM)

time: 116 us -> 91 us (0.78)
  Pallas kernels: 38.4 us -> 13.2 us
    pallas_call x1, Pallas kernels: 14.9 us -> 4.75 us  [local(): pl.pallas_call(first_kernel, out_shape=STATE, in_specs=[SM, VM, VM, VM],...]
    pallas_call x1, Pallas kernels: 8.72 us -> 2.94 us  [local(): pl.pallas_call(third_kernel, out_shape=STATE, in_specs=[SM, VM, VM, VM, V...]
    pallas_call x1, Pallas kernels: 5.88 us -> 2.38 us  [local(): pl.pallas_call(second_kernel, out_shape=STATE, in_specs=[SM, VM, VM, VM],...]
    pallas_call x1, Pallas kernels: 4.88 us -> 1.83 us  [local(): pl.pallas_call(leaf_kernel, out_shape=STATE, in_specs=[VM, VM], out_specs...]
    pallas_call x1, Pallas kernels: 4.04 us -> 1.26 us  [local(): pl.pallas_call(expand_kernel, out_shape=jax.ShapeDtypeStruct(shaped, jnp....]
  transfers between devices with their start and end apart: 4 -> 4, of which waited for: 4 -> 4; matrix products, arithmetic and copies ran while one was open for 6% -> 7% of each run, Pallas kernels for 0% -> 0%
where the time goes in v2:
time: 91 us; the launch traced here: 90 us
  waiting for transfers between devices  45.8 us (50%)
  starting transfers between devices  18.2 us (20%)
  Pallas kernels  13.2 us (15%)
  local copies, waits for them, and re-layouts  12 us (13%)
    all_to_all x1, waiting for transfers between devices, local(): state = lax.all_to_all(state, ('yl', 'z'), 0, 0, tiled=True)  15 us
    all_to_all x1, waiting for transfers between devices, local(): state = lax.all_to_all(state, ('yh', 'x'), 0, 0, tiled=True)  14.6 us
    all_to_all x1, waiting for transfers between devices, local(): state = lax.all_to_all(state, CHIPS, 0, 0, tiled=True)  13.5 us
    all_to_all x1, starting transfers between devices, local(): state = lax.all_to_all(state, CHIPS, 0, 0, tiled=True)  7.21 us
    all_to_all x1, starting transfers between devices, local(): state = lax.all_to_all(state, ('yh', 'x'), 0, 0, tiled=True)  7.01 us
    unnamed x15, local copies, waits for them, and re-layouts  5.65 us
    pallas_call x1, Pallas kernels, local(): pl.pallas_call(first_kernel, out_shape=STATE, in_specs=[SM, VM, VM, VM],...  4.75 us
    all_to_all x1, starting transfers between devices, local(): state = lax.all_to_all(state, ('yl', 'z'), 0, 0, tiled=True)  3.69 us
  transfers between devices with their start and end apart: 4, of which 4 were waited for; matrix products, arithmetic and copies ran while one was open for 7% of the time, Pallas kernels for 0%

profile of v2, /device:TPU:0, one launch (start us, length us, event | category | flops | bytes accessed | tf_op | source)
XLA Modules:
  0.0 90.0 jit_solution(11295794495719015220)
XLA Ops:
  0.0 1.5 %copy.7 = bf16[16,8,32,128]{3,2,1,0:T(8,128)(2,1)S(1)} copy(bf16[16,8,32,128]{3,1,2,0:T(8,128)(2,1)} %bitcast.19) | data formatting | bytes 2097152
  1.8 1.8 %shard_map.55 = bf16[64,64,128]{2,1,0:T(8,128)(2,1)} custom-call(bf16[128,32,128]{2,1,0:T(8,128)(2,1)S(1)} %bitcast.16, bf16[128,32,128]{2,1,0:T(8,128)(2,1)S(1)} %bitcast.17), custom_call_target="tpu_custom_call" | custom-call | tf_op jit(solution)/shard_map/pallas_call | solution.py:153
  3.6 7.0 %all-to-all-start = ((bf16[64,64,128]{2,1,0:T(8,128)(2,1)}), bf16[64,64,128]{2,1,0:T(8,128)(2,1)S(1)}, u32[]{:S(2)}, u32[]{:S(2)}) async-start(bf16[64,64,128]{2,1,0:T(8,128)(2,1)} %shard_map.55), calls=%async_computation | async-start | bytes 2097152 | tf_op jit(solution)/shard_map/all_to_all | solution.py:156
  10.7 1.0 %slice-done = s32[7,16384]{1,0:T(8,128)S(1)} async-done(((s32[14,16384]{1,0:T(8,128)}), s32[7,16384]{1,0:T(8,128)S(1)}, s32[]{:S(2)}) %slice-start) | async-done | bytes 458776 | tf_op jit(solution)/shard_map/slice | solution.py:145
  11.7 0.3 copy.14
  12.1 0.5 fusion
  12.6 0.6 pad_maximum_fusion.swapped
  13.2 14.6 %all-to-all-done.state = bf16[64,64,128]{2,1,0:T(8,128)(2,1)S(1)} async-done(((bf16[64,64,128]{2,1,0:T(8,128)(2,1)}), bf16[64,64,128]{2,1,0:T(8,128)(2,1)S(1)}, u32[]{:S(2)}, u32[]{:S(2)}) %all-to-all-start) | async-done | bytes 1048608 | tf_op jit(solution)/shard_map/all_to_all | solution.py:156
  27.9 4.7 %shard_map.56 = bf16[64,64,128]{2,1,0:T(8,128)(2,1)S(1)} custom-call(s32[896]{0:T(1024)S(1)} %reshape.27.chosen_ref, bf16[64,64,128]{2,1,0:T(8,128)(2,1)S(1)} %all-to-all-done.state, bf16[64,64,128]{2,1,0:T(8,128)(2,1)S(1)} %copy-done, bf16[64,64,128]{2,1,0:T(8,128)(2,1)S(1)} %pad_maximum_fusion.swapped), custom_call_target="tpu_custom_call" | custom-call | tf_op jit(solution)/shard_map/pallas_call | solution.py:157
  32.6 1.0 %copy-done.1 = bf16[64,64,128]{2,1,0:T(8,128)(2,1)} copy-done((bf16[64,64,128]{2,1,0:T(8,128)(2,1)}, bf16[64,64,128]{2,1,0:T(8,128)(2,1)S(1)}, u32[]{:S(2)}) %copy-start.1) | copy-done | bytes 1048600
  33.6 7.2 %all-to-all-start.1 = ((bf16[64,64,128]{2,1,0:T(8,128)(2,1)}), bf16[64,64,128]{2,1,0:T(8,128)(2,1)S(1)}, u32[]{:S(2)}, u32[]{:S(2)}) async-start(bf16[64,64,128]{2,1,0:T(8,128)(2,1)} %copy-done.1), calls=%async_computation.1 | async-start | bytes 2097152 | tf_op jit(solution)/shard_map/all_to_all | solution.py:161
  40.8 1.0 %constant_dynamic-slice_fusion.1 = s32[7,2048]{1,0:T(8,128)S(1)} fusion(s32[14,16384]{1,0:T(8,128)} %param.8, s32[]{:T(128)S(6)} %select_n.12), kind=kLoop, calls=%fused_computation.5 | loop fusion | bytes 114692 | tf_op jit(solution)/shard_map/dynamic_slice | solution.py:147
  41.8 1.4 %reshape.24 = s32[7,8,2,16,8]{4,3,2,1,0:T(8,128)} reshape(s32[7,2048]{1,0:T(8,128)S(1)} %constant_dynamic-slice_fusion.1) | data formatting | bytes 114688 | tf_op jit(solution)/shard_map/reshape | solution.py:149
  43.2 2.2 %dynamic-slice_reduce_fusion = s32[7,8,16]{2,1,0:T(8,128)S(1)} fusion(s32[7,8,2,16,8]{4,3,2,1,0:T(8,128)} %reshape.24, s32[]{:T(128)S(6)} %select_n.13, s32[]{:T(128)S(6)} %select_n.14), kind=kLoop, calls=%fused_computation.3 | loop fusion | bytes 7176 | tf_op jit(solution)/shard_map/dynamic_slice | solution.py:148
  45.5 13.5 %all-to-all-done.1.state = bf16[64,64,128]{2,1,0:T(8,128)(2,1)S(1)} async-done(((bf16[64,64,128]{2,1,0:T(8,128)(2,1)}), bf16[64,64,128]{2,1,0:T(8,128)(2,1)S(1)}, u32[]{:S(2)}, u32[]{:S(2)}) %all-to-all-start.1) | async-done | bytes 1048608 | tf_op jit(solution)/shard_map/all_to_all | solution.py:161
  59.0 2.4 %shard_map.57.state = bf16[64,64,128]{2,1,0:T(8,128)(2,1)S(1)} custom-call(s32[896]{0:T(1024)S(1)} %reshape.25.chosen_ref, bf16[64,64,128]{2,1,0:T(8,128)(2,1)S(1)} %all-to-all-done.1.state, bf16[64,64,128]{2,1,0:T(8,128)(2,1)S(1)} %copy-done, bf16[64,64,128]{2,1,0:T(8,128)(2,1)S(1)} %pad_maximum_fusion.swapped), custom_call_target="tpu_custom_call" | custom-call | tf_op jit(solution)/shard_map/pallas_call | solution.py:162
  61.4 0.3 collective-permute-start
  61.7 2.6 %collective-permute-done.partner = bf16[64,64,128]{2,1,0:T(8,128)(2,1)S(1)} collective-permute-done((bf16[64,64,128]{2,1,0:T(8,128)(2,1)S(1)}, bf16[64,64,128]{2,1,0:T(8,128)(2,1)S(1)}, u32[]{:S(2)}, u32[]{:S(2)}) %collective-permute-start) | collective-permute-done | bytes 1048608 | tf_op jit(solution)/shard_map/ppermute | solution.py:166
  64.3 2.9 %shard_map.58 = bf16[64,64,128]{2,1,0:T(8,128)(2,1)S(1)} custom-call(s32[896]{0:T(1024)S(1)} %reshape.25.chosen_ref, bf16[64,64,128]{2,1,0:T(8,128)(2,1)S(1)} %shard_map.57.state, bf16[64,64,128]{2,1,0:T(8,128)(2,1)S(1)} %collective-permute-done.partner, bf16[64,64,128]{2,1,0:T(8,128)(2,1)S(1)} %copy-done, bf16[64,64,128]{2,1,0:T(8,128)(2,1)S(1)} %pad_maximum_fusion.swapped), custom_call_target="tpu_custom_call" | custom-call | tf_op jit(solution)/shard_map/pallas_call | solution.py:167
  67.3 1.0 %copy-done.2 = bf16[64,64,128]{2,1,0:T(8,128)(2,1)} copy-done((bf16[64,64,128]{2,1,0:T(8,128)(2,1)}, bf16[64,64,128]{2,1,0:T(8,128)(2,1)S(1)}, u32[]{:S(2)}) %copy-start.2) | copy-done | bytes 1048600
  68.3 3.7 %all-to-all-start.2 = ((bf16[64,64,128]{2,1,0:T(8,128)(2,1)}), bf16[64,64,128]{2,1,0:T(8,128)(2,1)S(1)}, u32[]{:S(2)}, u32[]{:S(2)}) async-start(bf16[64,64,128]{2,1,0:T(8,128)(2,1)} %copy-done.2), calls=%async_computation.2 | async-start | bytes 2097152 | tf_op jit(solution)/shard_map/all_to_all | solution.py:171
  72.2 15.0 %all-to-all-done.2.state = bf16[64,64,128]{2,1,0:T(8,128)(2,1)S(1)} async-done(((bf16[64,64,128]{2,1,0:T(8,128)(2,1)}), bf16[64,64,128]{2,1,0:T(8,128)(2,1)S(1)}, u32[]{:S(2)}, u32[]{:S(2)}) %all-to-all-start.2) | async-done | bytes 1048608 | tf_op jit(solution)/shard_map/all_to_all | solution.py:171
  87.3 1.3 %shard_map.59 = bf16[128,32,128]{2,1,0:T(8,128)(2,1)S(1)} custom-call(bf16[64,64,128]{2,1,0:T(8,128)(2,1)S(1)} %all-to-all-done.2.state, bf16[128,32,128]{2,1,0:T(8,128)(2,1)S(1)} %bitcast.14), custom_call_target="tpu_custom_call" | custom-call | tf_op jit(solution)/shard_map/pallas_call | solution.py:172
  88.5 1.4 %copy.13 = bf16[16,8,32,128]{3,1,2,0:T(8,128)(2,1)} copy(bf16[16,8,32,128]{3,2,1,0:T(8,128)(2,1)S(1)} %bitcast.15) | data formatting | bytes 2097152
  (14 shorter events, 0.7 us)
Async XLA Ops:
  0.0 1.5 %copy-start.3 = (bf16[128,4096]{1,0:T(8,128)(2,1)S(1)}, bf16[128,4096]{1,0:T(8,128)(2,1)}, u32[]{:S(2)}) copy-start(bf16[128,4096]{1,0:T(8,128)(2,1)} %param.5) | copy-start | bytes 3145732
  3.6 24.2 %all-to-all-start = ((bf16[64,64,128]{2,1,0:T(8,128)(2,1)}), bf16[64,64,128]{2,1,0:T(8,128)(2,1)S(1)}, u32[]{:S(2)}, u32[]{:S(2)}) async-start(bf16[64,64,128]{2,1,0:T(8,128)(2,1)} %shard_map.55), calls=%async_computation | async-start | bytes 2097152 | tf_op jit(solution)/shard_map/all_to_all | solution.py:156
  10.7 1.0 %slice-start = ((s32[14,16384]{1,0:T(8,128)}), s32[7,16384]{1,0:T(8,128)S(1)}, s32[]{:S(2)}) async-start(s32[14,16384]{1,0:T(8,128)} %param.8), calls=%async_computation.3 | async-start | bytes 1048576 | tf_op jit(solution)/shard_map/slice | solution.py:145
  10.7 1.5 %copy-start = (bf16[64,64,128]{2,1,0:T(8,128)(2,1)S(1)}, bf16[64,64,128]{2,1,0:T(8,128)(2,1)}, u32[]{:S(2)}) copy-start(bf16[64,64,128]{2,1,0:T(8,128)(2,1)} %near.5) | copy-start | bytes 3145732
  32.6 1.0 %copy-start.1 = (bf16[64,64,128]{2,1,0:T(8,128)(2,1)}, bf16[64,64,128]{2,1,0:T(8,128)(2,1)S(1)}, u32[]{:S(2)}) copy-start(bf16[64,64,128]{2,1,0:T(8,128)(2,1)S(1)} %shard_map.56) | copy-start | bytes 3145732
  33.6 25.4 %all-to-all-start.1 = ((bf16[64,64,128]{2,1,0:T(8,128)(2,1)}), bf16[64,64,128]{2,1,0:T(8,128)(2,1)S(1)}, u32[]{:S(2)}, u32[]{:S(2)}) async-start(bf16[64,64,128]{2,1,0:T(8,128)(2,1)} %copy-done.1), calls=%async_computation.1 | async-start | bytes 2097152 | tf_op jit(solution)/shard_map/all_to_all | solution.py:161
  61.4 2.9 %collective-permute-start = (bf16[64,64,128]{2,1,0:T(8,128)(2,1)S(1)}, bf16[64,64,128]{2,1,0:T(8,128)(2,1)S(1)}, u32[]{:S(2)}, u32[]{:S(2)}) collective-permute-start(bf16[64,64,128]{2,1,0:T(8,128)(2,1)S(1)} %shard_map.57.state), channel_id=1, source_target_pairs={{0,1},{1,0},{2,3},{3,2},{4,5},{5,4},{6,7},{7,6},{8,9},{9,8},{10,11... | collective-permute-start | bytes 3145736 | tf_op jit(solution)/shard_map/ppermute | solution.py:166
  67.3 1.0 %copy-start.2 = (bf16[64,64,128]{2,1,0:T(8,128)(2,1)}, bf16[64,64,128]{2,1,0:T(8,128)(2,1)S(1)}, u32[]{:S(2)}) copy-start(bf16[64,64,128]{2,1,0:T(8,128)(2,1)S(1)} %shard_map.58) | copy-start | bytes 3145732
  68.3 3.7 %copy-start.4 = (bf16[128,4096]{1,0:T(8,128)(2,1)S(1)}, bf16[128,4096]{1,0:T(8,128)(2,1)}, u32[]{:S(2)}) copy-start(bf16[128,4096]{1,0:T(8,128)(2,1)} %param.7) | copy-start | bytes 3145732
  68.3 19.0 %all-to-all-start.2 = ((bf16[64,64,128]{2,1,0:T(8,128)(2,1)}), bf16[64,64,128]{2,1,0:T(8,128)(2,1)S(1)}, u32[]{:S(2)}, u32[]{:S(2)}) async-start(bf16[64,64,128]{2,1,0:T(8,128)(2,1)} %copy-done.2), calls=%async_computation.2 | async-start | bytes 2097152 | tf_op jit(solution)/shard_map/all_to_all | solution.py:171

commit v3 on v2

v3 whole, which is shorter than its diff:
```python
import functools

import jax
import jax.numpy as jnp
from jax import lax
from jax.experimental import pallas as pl
from jax.experimental.pallas import tpu as pltpu
from jax.sharding import Mesh, PartitionSpec as P

LEAF = 64
RANK = 64
VECS = 64
WIDE = 2 * VECS
TILES = 64
AXES = ("yh", "x", "yl", "z", "core")
CHIPS = ("yh", "x", "yl", "z")


def left_half(shape):
    return lax.broadcasted_iota(jnp.int32, shape, len(shape) - 1) < VECS


def halves(tile):
    left = left_half(tile.shape)
    zero = jnp.zeros_like(tile)
    return jnp.where(left, tile, zero), jnp.where(left, zero, tile)


def swap_halves(tile):
    return jnp.concatenate([tile[:, VECS:], tile[:, :VECS]], axis=1)


def dot(lhs, rhs):
    return jnp.dot(lhs, rhs, preferred_element_type=jnp.float32).astype(jnp.bfloat16)


def tile_level(load, store, near, swapped, chosen, bit, tiles):
    for a in tiles:
        if a >> bit & 1:
            continue
        b = a + (1 << bit)
        al, ar = halves(load(a))
        bl, br = halves(load(b))
        weights = jnp.concatenate([al, bl, ar, br], axis=0)
        for_a = jnp.concatenate([near[chosen(a, 0)], near[chosen(a, 1)]], axis=1)
        for_b = jnp.concatenate([swapped[chosen(b, 0)], swapped[chosen(b, 1)]], axis=1)
        out = dot(jnp.concatenate([for_a, for_b], axis=0), weights)
        store(a, out[:RANK])
        store(b, out[RANK:])


def lane_level(load, store, near, chosen, tiles):
    for a in tiles:
        tile = load(a)
        al, ar = halves(tile)
        bl, br = halves(swap_halves(tile))
        weights = jnp.concatenate([al, bl, ar, br], axis=0)
        store(a, dot(jnp.concatenate([near[chosen(a, 0)], near[chosen(a, 1)]], axis=1), weights))


def other_level(load, load_partner, store, near, chosen, tiles):
    for a in tiles:
        al, ar = halves(load(a))
        bl, br = halves(load_partner(a))
        weights = jnp.concatenate([al, bl, ar, br], axis=0)
        store(a, dot(jnp.concatenate([near[chosen(a, 0)], near[chosen(a, 1)]], axis=1), weights))


def getter(ref):
    return lambda tile: ref[tile]


def setter(ref):
    def store(tile, value):
        ref[tile] = value

    return store


def col_place():
    return lax.axis_index("yh") * 4 + lax.axis_index("x")


def row_low():
    return lax.axis_index("yl") * 4 + lax.axis_index("z")


def leaf_kernel(maps, vectors, out, v_in, x_in, made, v_sem, x_sem, out_sem):
    copies = []
    for n in range(2):
        rows = pl.ds(n * 64, 64)
        copies.append(
            (
                pltpu.make_async_copy(maps.at[rows], v_in.at[rows], v_sem.at[n]),
                pltpu.make_async_copy(vectors.at[rows], x_in.at[rows], x_sem.at[n]),
            )
        )
        for copy in copies[-1]:
            copy.start()
    zero = jnp.zeros((LEAF // 2, WIDE), jnp.bfloat16)
    sent = []
    for h in range(8):
        if h % 4 == 0:
            for copy in copies[h // 4]:
                copy.wait()
        rows = pl.ds(h * 16, 16)
        maps_here = v_in[rows].reshape(16, LEAF // 2, WIDE)
        vectors_here = x_in[rows].reshape(16, LEAF // 2, WIDE)
        for tile in range(0, 8, 2):
            order = [tile + step for step in (0, 8, 1, 9)]
            v = jnp.concatenate([maps_here[j] for j in order], axis=0).T
            lhs = jnp.concatenate([v[:RANK], v[RANK:]], axis=1)
            even, odd = [], []
            for place, j in enumerate(order):
                raw = vectors_here[j]
                el, orr = halves(raw)
                ol, er = halves(swap_halves(raw))
                e, o = (el, ol) if place % 2 == 0 else (er, orr)
                even.append([e, zero] if place < 2 else [zero, e])
                odd.append([o, zero] if place < 2 else [zero, o])
            weights = jnp.concatenate([jnp.concatenate(r, axis=1) for r in even + odd], axis=0)
            both = dot(lhs, weights)
            made[h * 8 + tile] = both[:, :WIDE]
            made[h * 8 + tile + 1] = both[:, WIDE:]
        if h % 4 == 3:
            done = pl.ds((h - 3) * 8, 32)
            sent.append(pltpu.make_async_copy(made.at[done], out.at[done], out_sem.at[h // 4]))
            sent[-1].start()
    for copy in sent:
        copy.wait()


def table_kernel(
    patterns, late_patterns, translations, first_chosen, second_chosen, near, swapped, p_in, p_sem, t_sem
):
    table = pltpu.make_async_copy(translations, near, t_sem)
    table.start()
    core = lax.axis_index("core")
    lookups = []
    for k in range(8):
        columns = pl.ds(pl.multiple_of((k * 16 + row_low() * 2 + core) * 128, 128), 128)
        lookups.append(pltpu.make_async_copy(patterns.at[pl.ds(0, 8), columns], p_in.at[k], p_sem.at[k]))
        lookups[k].start()
    lane = lax.broadcasted_iota(jnp.int32, (8, 128), 1)
    first = second = jnp.zeros((8, 128), jnp.int32)
    for k in range(8):
        turn = jnp.remainder(k - row_low() + 128, 128)
        rows = late_patterns[:, pl.ds(pl.multiple_of((k * 2 + core) * 128, 128), 128)]
        second = jnp.where((lane & 7) == k, pltpu.roll(rows, turn, 1), second)
    second_chosen[...] = second
    for k in range(8):
        lookups[k].wait()
    for k in range(8):
        turn = jnp.remainder((k - col_place()) * 16 + 128, 128)
        first = jnp.where((lane >> 4) == k, pltpu.roll(p_in[k], turn, 1), first)
    first_chosen[...] = first
    table.wait()
    for m in range(near.shape[0]):
        swapped[m] = swap_halves(near[m])


def lookup(chosen_ref, level):
    return lambda tile, half: chosen_ref[level, (tile >> 3) * 16 + half * 8 + (tile & 7)]


def first_kernel(chosen_ref, state, near, swapped, out, one, two):
    every = range(TILES)
    bufs = [state, one, two, one, two, one, two]
    for level, bit in enumerate((3, 4, 5, 0, 1, 2)):
        tile_level(
            getter(bufs[level]), setter(bufs[level + 1]), near, swapped, lookup(chosen_ref, level), bit, every
        )
    lane_level(getter(two), setter(out), near, lookup(chosen_ref, 6), every)


HALVES = [[tile for tile in range(TILES) if tile >> 2 & 1 == n] for n in range(2)]


def packed(tile):
    return (tile >> 3) * 4 + (tile & 3)


def second_kernel(part, chosen_ref, state, near, swapped, out, one, two):
    tiles = HALVES[part]

    def store_out(tile, value):
        out[packed(tile)] = value

    loads = [getter(state), getter(one), getter(two)]
    stores = [setter(one), setter(two), store_out]
    for level in range(3):
        tile_level(
            loads[level], stores[level], near, swapped, lookup(chosen_ref, 1 + level), 3 + level, tiles
        )


def row_levels(part, chosen_ref, state, partner, near, swapped, one, two, store):
    tiles = HALVES[part]
    load, load_partner = (lambda tile, ref=ref: ref[packed(tile)] for ref in (state, partner))
    other_level(load, load_partner, setter(one), near, lookup(chosen_ref, 4), tiles)
    tile_level(getter(one), setter(two), near, swapped, lookup(chosen_ref, 5), 0, tiles)
    tile_level(getter(two), store, near, swapped, lookup(chosen_ref, 6), 1, tiles)


def third_kernel(chosen_ref, state, partner, near, swapped, out, one, two):
    def store(tile, value):
        out[packed(tile)] = value

    row_levels(0, chosen_ref, state, partner, near, swapped, one, two, store)


def fourth_kernel(chosen_ref, earlier, state, partner, near, swapped, out, one, two):
    row_levels(1, chosen_ref, state, partner, near, swapped, one, two, setter(one))
    load = lambda tile: one[tile] if tile >> 2 & 1 else earlier[packed(tile)]

    def store(tile, value):
        out[(tile & 7) * 8 + (tile >> 3)] = value

    tile_level(load, store, near, swapped, lookup(chosen_ref, 7), 2, range(TILES))


def expand_kernel(state, maps, out, made, sem):
    copies = []
    zero = jnp.zeros((LEAF // 2, WIDE), jnp.bfloat16)
    for h in range(8):
        rows = pl.ds(h * 16, 16)
        maps_here = maps[rows].reshape(16, LEAF // 2, WIDE)
        results = [None] * 16
        for q in range(8):
            both = state[q * 8 + h]
            al, ar = halves(both)
            bl, br = halves(swap_halves(both))
            lhs = [[maps_here[q], zero], [zero, maps_here[q + 8]]]
            lhs = jnp.concatenate([jnp.concatenate(r, axis=1) for r in lhs], axis=0)
            two = dot(lhs, jnp.concatenate([al, br, bl, ar], axis=0))
            results[q], results[q + 8] = two[: LEAF // 2], two[LEAF // 2 :]
        made[rows] = jnp.stack(results, axis=0).reshape(16, LEAF * VECS)
        copies.append(pltpu.make_async_copy(made.at[rows], out.at[rows], sem.at[h]))
        copies[-1].start()
    for copy in copies:
        copy.wait()


VM = pl.BlockSpec(memory_space=pltpu.VMEM)
SM = pl.BlockSpec(memory_space=pltpu.SMEM)
HB = pl.BlockSpec(memory_space=pltpu.HBM)
PARAMS = pltpu.CompilerParams(vmem_limit_bytes=32 * 1024 * 1024)
STATE = jax.ShapeDtypeStruct((TILES, RANK, WIDE), jnp.bfloat16)
HALF = jax.ShapeDtypeStruct((TILES // 2, RANK, WIDE), jnp.bfloat16)


def make_tables(patterns, translations):
    late_patterns = lax.dynamic_slice(patterns, (6, col_place() * 2048), (8, 2048))
    table = jax.ShapeDtypeStruct(translations.shape, translations.dtype)
    return pl.pallas_call(
        table_kernel,
        out_shape=[
            jax.ShapeDtypeStruct((8, 128), jnp.int32), jax.ShapeDtypeStruct((8, 128), jnp.int32), table, table,
        ],
        in_specs=[HB, VM, HB], out_specs=[VM] * 4,
        scratch_shapes=[
            pltpu.VMEM((8, 8, 128), jnp.int32), pltpu.SemaphoreType.DMA((8,)), pltpu.SemaphoreType.DMA,
        ],
        compiler_params=PARAMS,
    )(patterns, late_patterns, translations)


def local(inputs, leaf_maps, expand_maps, patterns, translations):
    rows = jax.ShapeDtypeStruct(inputs.shape, jnp.bfloat16)
    scratch = [pltpu.VMEM(STATE.shape, STATE.dtype)] * 2
    state = pl.pallas_call(
        leaf_kernel, out_shape=STATE, in_specs=[HB] * 2, out_specs=HB,
        scratch_shapes=[pltpu.VMEM(rows.shape, rows.dtype)] * 2
        + [pltpu.VMEM(STATE.shape, STATE.dtype)] + [pltpu.SemaphoreType.DMA((2,))] * 3,
        compiler_params=pltpu.CompilerParams(vmem_limit_bytes=63 * 1024 * 1024),
    )(leaf_maps, inputs)
    first_chosen, second_chosen, near, swapped = make_tables(patterns, translations)
    state = lax.all_to_all(state, ("yh", "x"), 0, 0, tiled=True)
    state = pl.pallas_call(
        first_kernel, out_shape=STATE, in_specs=[SM, VM, VM, VM], out_specs=VM,
        scratch_shapes=scratch, compiler_params=PARAMS,
    )(first_chosen, state, near, swapped)
    state = lax.all_to_all(state, CHIPS, 0, 0, tiled=True)
    parts, partners = [], []
    for n in range(2):
        parts.append(
            pl.pallas_call(
                functools.partial(second_kernel, n), out_shape=HALF, in_specs=[SM, VM, VM, VM], out_specs=VM,
                scratch_shapes=scratch, compiler_params=PARAMS,
            )(second_chosen, state, near, swapped)
        )
        partners.append(lax.ppermute(parts[n], "core", [(0, 1), (1, 0)]))
    earlier = pl.pallas_call(
        third_kernel, out_shape=HALF, in_specs=[SM, VM, VM, VM, VM], out_specs=VM,
        scratch_shapes=scratch, compiler_params=PARAMS,
    )(second_chosen, parts[0], partners[0], near, swapped)
    state = pl.pallas_call(
        fourth_kernel, out_shape=STATE, in_specs=[SM, VM, VM, VM, VM, VM], out_specs=VM,
        scratch_shapes=scratch, compiler_params=PARAMS,
    )(second_chosen, earlier, parts[1], partners[1], near, swapped)
    state = lax.all_to_all(state, ("yl", "z"), 0, 0, tiled=True)
    return pl.pallas_call(
        expand_kernel, out_shape=rows, in_specs=[VM, VM], out_specs=HB,
        scratch_shapes=[pltpu.VMEM(rows.shape, rows.dtype), pltpu.SemaphoreType.DMA((8,))],
        compiler_params=PARAMS,
    )(state, expand_maps)


def solution(mesh):
    fine = Mesh(mesh.devices.reshape(2, 4, 2, 4, 2), AXES)
    rows = P(AXES, None)
    return jax.shard_map(
        local, mesh=fine, in_specs=(rows, rows, rows, P(), P()), out_specs=rows, check_vma=False
    )
```

time: 91 us -> 86.7 us (0.953)
  blocking collectives: 0 us -> 44.1 us
  waiting for transfers between devices: 45.8 us -> 13 us
  starting transfers between devices: 18.2 us -> 7.86 us
  local copies, waits for them, and re-layouts: 12 us -> 3.44 us
  Pallas kernels: 13.2 us -> 17.6 us
    all_to_all x0 -> x2, blocking collectives: none -> 44.1 us  [the longest x1 25.2 us: local(): state = lax.all_to_all(state, CHIPS, 0, 0, tiled=True)]
    all_to_all x2 -> x0, waiting for transfers between devices: 28.6 us -> none  [the longest x1 15 us: local(): state = lax.all_to_all(state, ('yl', 'z'), 0, 0, tiled=True)]
    all_to_all x2 -> x0, starting transfers between devices: 10.9 us -> none  [the longest x1 7.21 us: local(): state = lax.all_to_all(state, CHIPS, 0, 0, tiled=True)]
    pallas_call x4 -> x7, Pallas kernels: 8.41 us -> 12.9 us  [the longest x1 3.36 us: local(): pl.pallas_call(leaf_kernel, out_shape=STATE, in_specs=[HB] * 2, out_specs...]
    unnamed x15 -> x6, local copies, waits for them, and re-layouts: 5.65 us -> 2.45 us
    ppermute x1 -> x2, waiting for transfers between devices: 2.65 us -> 0.01 us  [local(): partners.append(lax.ppermute(parts[n], 'core', [(0, 1), (1, 0)]))]
    dynamic_slice x3 -> x1, local copies, waits for them, and re-layouts: 3.26 us -> 0.99 us  [make_tables(): lax.dynamic_slice(patterns, (6, col_place() * 2048), (8, 2048))]
    all_to_all x1, waiting for transfers between devices: 14.6 us -> 13 us  [local(): state = lax.all_to_all(state, ('yh', 'x'), 0, 0, tiled=True)]
  transfers between devices with their start and end apart: 4 -> 3, of which waited for: 4 -> 1; matrix products, arithmetic and copies ran while one was open for 7% -> 1% of each run, Pallas kernels for 0% -> 5%
where the time goes in v3:
time: 86.7 us; the launch traced here: 86.3 us
  blocking collectives  44.1 us (51%)
  Pallas kernels  17.6 us (20%)
  waiting for transfers between devices  13 us (15%)
  starting transfers between devices  7.86 us (9%)
  local copies, waits for them, and re-layouts  3.44 us (4%)
    all_to_all x1, blocking collectives, local(): state = lax.all_to_all(state, CHIPS, 0, 0, tiled=True)  25.2 us
    all_to_all x1, blocking collectives, local(): state = lax.all_to_all(state, ('yl', 'z'), 0, 0, tiled=True)  18.9 us
    all_to_all x1, waiting for transfers between devices, local(): state = lax.all_to_all(state, ('yh', 'x'), 0, 0, tiled=True)  13 us
    all_to_all x1, starting transfers between devices, local(): state = lax.all_to_all(state, ('yh', 'x'), 0, 0, tiled=True)  7.03 us
    pallas_call x1, Pallas kernels, local(): pl.pallas_call(first_kernel, out_shape=STATE, in_specs=[SM, VM, VM, VM],...  4.75 us
    pallas_call x1, Pallas kernels, local(): pl.pallas_call(leaf_kernel, out_shape=STATE, in_specs=[HB] * 2, out_specs...  3.36 us
    pallas_call x2, Pallas kernels, local(): pl.pallas_call(functools.partial(second_kernel, n), out_shape=HALF, in_sp...  3.19 us
    unnamed x6, local copies, waits for them, and re-layouts  2.45 us
  transfers between devices with their start and end apart: 3, of which 1 were waited for; matrix products, arithmetic and copies ran while one was open for 1% of the time, Pallas kernels for 5%

profile of v3, /device:TPU:0, one launch (start us, length us, event | category | flops | bytes accessed | tf_op | source)
XLA Modules:
  0.0 86.3 jit_solution(6666894091186595720)
XLA Ops:
  0.0 3.4 %shard_map.56 = bf16[64,64,128]{2,1,0:T(8,128)(2,1)} custom-call(bf16[128,4096]{1,0:T(8,128)(2,1)} %maps.2, bf16[128,4096]{1,0:T(8,128)(2,1)} %vectors.1), custom_call_target="tpu_custom_call" | custom-call | tf_op jit(solution)/shard_map/pallas_call | solution.py:271
  3.4 7.0 %all-to-all-start = ((bf16[64,64,128]{2,1,0:T(8,128)(2,1)}), bf16[64,64,128]{2,1,0:T(8,128)(2,1)S(1)}, u32[]{:S(2)}, u32[]{:S(2)}) async-start(bf16[64,64,128]{2,1,0:T(8,128)(2,1)} %shard_map.56), calls=%async_computation | async-start | bytes 2097152 | tf_op jit(solution)/shard_map/all_to_all | solution.py:278
  10.4 1.0 %constant_dynamic-slice_fusion.late_patterns = s32[8,2048]{1,0:T(8,128)S(1)} fusion(s32[14,16384]{1,0:T(8,128)} %patterns.1, s32[]{:T(128)S(6)} %select_n.3), kind=kLoop, calls=%fused_computation | loop fusion | bytes 131076 | tf_op jit(solution)/shard_map/dynamic_slice | solution.py:253
  11.4 0.0 copy-start
  11.4 1.2 %copy-done = s32[14,16384]{1,0:T(8,128)S(1)} copy-done((s32[14,16384]{1,0:T(8,128)S(1)}, s32[14,16384]{1,0:T(8,128)}, u32[]{:S(2)}) %copy-start) | copy-done | bytes 917528
  12.6 0.0 copy-start.2
  12.6 1.2 %copy-done.2 = bf16[64,64,128]{2,1,0:T(8,128)(2,1)S(1)} copy-done((bf16[64,64,128]{2,1,0:T(8,128)(2,1)S(1)}, bf16[64,64,128]{2,1,0:T(8,128)(2,1)}, u32[]{:S(2)}) %copy-start.2) | copy-done | bytes 1048600
  13.8 0.8 shard_map.55
  14.6 13.0 %all-to-all-done.state = bf16[64,64,128]{2,1,0:T(8,128)(2,1)S(1)} async-done(((bf16[64,64,128]{2,1,0:T(8,128)(2,1)}), bf16[64,64,128]{2,1,0:T(8,128)(2,1)S(1)}, u32[]{:S(2)}, u32[]{:S(2)}) %all-to-all-start) | async-done | bytes 1048608 | tf_op jit(solution)/shard_map/all_to_all | solution.py:278
  27.6 4.7 %shard_map.57 = bf16[64,64,128]{2,1,0:T(8,128)(2,1)S(1)} custom-call(s32[8,128]{1,0:T(8,128)S(1)} %get-tuple-element.10.chosen_ref, bf16[64,64,128]{2,1,0:T(8,128)(2,1)S(1)} %all-to-all-done.state, bf16[64,64,128]{2,1,0:T(8,128)(2,1)S(1)} %get-tuple-element.11.near, bf16[64,64,128]{2,1,0:T(8,128)(2,1)S(1)} %get-tuple-element.12.swapped), custom_call_target="tpu_custom_call" | custom-call | tf_op jit(solution)/shard_map/pallas_call | solution.py:279
  32.4 25.2 %all_to_all.15.state = bf16[64,64,128]{2,1,0:T(8,128)(2,1)S(1)} all-to-all(bf16[64,64,128]{2,1,0:T(8,128)(2,1)S(1)} %shard_map.57), channel_id=1, replica_groups=mesh['yh'=2,'x'=4,'yl'=2,'z'=4,'core'=2] {'yh','x','yl','z'}, dimensions={0} | all-to-all | bytes 2097152 | tf_op jit(solution)/shard_map/all_to_all | solution.py:283
  57.6 1.6 %shard_map.58.state = bf16[32,64,128]{2,1,0:T(8,128)(2,1)S(1)} custom-call(s32[8,128]{1,0:T(8,128)S(1)} %get-tuple-element.9.chosen_ref, bf16[64,64,128]{2,1,0:T(8,128)(2,1)S(1)} %all_to_all.15.state, bf16[64,64,128]{2,1,0:T(8,128)(2,1)S(1)} %get-tuple-element.11.near, bf16[64,64,128]{2,1,0:T(8,128)(2,1)S(1)} %get-tuple-element.12.swapped), custom_call_target="tpu_custom_call" | custom-call | tf_op jit(solution)/shard_map/pallas_call | solution.py:287
  59.2 0.1 collective-permute-start
  59.3 1.6 %shard_map.60.state = bf16[32,64,128]{2,1,0:T(8,128)(2,1)S(1)} custom-call(s32[8,128]{1,0:T(8,128)S(1)} %get-tuple-element.9.chosen_ref, bf16[64,64,128]{2,1,0:T(8,128)(2,1)S(1)} %all_to_all.15.state, bf16[64,64,128]{2,1,0:T(8,128)(2,1)S(1)} %get-tuple-element.11.near, bf16[64,64,128]{2,1,0:T(8,128)(2,1)S(1)} %get-tuple-element.12.swapped), custom_call_target="tpu_custom_call" | custom-call | tf_op jit(solution)/shard_map/pallas_call | solution.py:287
  60.9 0.8 collective-permute-start.1
  61.7 0.0 collective-permute-done.partner
  61.7 1.6 %shard_map.59.earlier = bf16[32,64,128]{2,1,0:T(8,128)(2,1)S(1)} custom-call(s32[8,128]{1,0:T(8,128)S(1)} %get-tuple-element.9.chosen_ref, bf16[32,64,128]{2,1,0:T(8,128)(2,1)S(1)} %shard_map.58.state, bf16[32,64,128]{2,1,0:T(8,128)(2,1)S(1)} %collective-permute-done.partner, bf16[64,64,128]{2,1,0:T(8,128)(2,1)S(1)} %get-tuple-element.11.near, ...), custom_call_target="tpu_custom_call" | custom-call | tf_op jit(solution)/shard_map/pallas_call | solution.py:293
  63.3 0.0 collective-permute-done.1.partner
  63.3 2.1 %shard_map.61 = bf16[64,64,128]{2,1,0:T(8,128)(2,1)S(1)} custom-call(s32[8,128]{1,0:T(8,128)S(1)} %get-tuple-element.9.chosen_ref, bf16[32,64,128]{2,1,0:T(8,128)(2,1)S(1)} %shard_map.59.earlier, bf16[32,64,128]{2,1,0:T(8,128)(2,1)S(1)} %shard_map.60.state, bf16[32,64,128]{2,1,0:T(8,128)(2,1)S(1)} %collective-permute-done.1.partner, ...), custom_call_target="tpu_custom_call" | custom-call | tf_op jit(solution)/shard_map/pallas_call | solution.py:297
  65.4 0.0 copy-start.1
  65.4 18.9 %all_to_all.16.state = bf16[64,64,128]{2,1,0:T(8,128)(2,1)S(1)} all-to-all(bf16[64,64,128]{2,1,0:T(8,128)(2,1)S(1)} %shard_map.61), channel_id=1, replica_groups=mesh['yh'=2,'x'=4,'yl'=2,'z'=4,'core'=2] {'yl','z'}, dimensions={0} | all-to-all | bytes 2097152 | tf_op jit(solution)/shard_map/all_to_all | solution.py:301
  84.3 0.0 copy-done.1
  84.3 1.8 %shard_map.62 = bf16[128,4096]{1,0:T(8,128)(2,1)} custom-call(bf16[64,64,128]{2,1,0:T(8,128)(2,1)S(1)} %all_to_all.16.state, bf16[128,4096]{1,0:T(8,128)(2,1)S(1)} %copy-done.1), custom_call_target="tpu_custom_call" | custom-call | tf_op jit(solution)/shard_map/pallas_call | solution.py:302
Async XLA Ops:
  3.4 24.2 %all-to-all-start = ((bf16[64,64,128]{2,1,0:T(8,128)(2,1)}), bf16[64,64,128]{2,1,0:T(8,128)(2,1)S(1)}, u32[]{:S(2)}, u32[]{:S(2)}) async-start(bf16[64,64,128]{2,1,0:T(8,128)(2,1)} %shard_map.56), calls=%async_computation | async-start | bytes 2097152 | tf_op jit(solution)/shard_map/all_to_all | solution.py:278
  11.4 1.2 %copy-start = (s32[14,16384]{1,0:T(8,128)S(1)}, s32[14,16384]{1,0:T(8,128)}, u32[]{:S(2)}) copy-start(s32[14,16384]{1,0:T(8,128)} %patterns.1) | copy-start | bytes 2752516
  12.6 1.2 %copy-start.2 = (bf16[64,64,128]{2,1,0:T(8,128)(2,1)S(1)}, bf16[64,64,128]{2,1,0:T(8,128)(2,1)}, u32[]{:S(2)}) copy-start(bf16[64,64,128]{2,1,0:T(8,128)(2,1)} %translations.1) | copy-start | bytes 3145732
  59.2 2.5 %collective-permute-start = (bf16[32,64,128]{2,1,0:T(8,128)(2,1)S(1)}, bf16[32,64,128]{2,1,0:T(8,128)(2,1)S(1)}, u32[]{:S(2)}, u32[]{:S(2)}) collective-permute-start(bf16[32,64,128]{2,1,0:T(8,128)(2,1)S(1)} %shard_map.58.state), channel_id=1, source_target_pairs={{0,1},{1,0},{2,3},{3,2},{4,5},{5,4},{6,7},{7,6},{8,9},{9,8},{10,11... | collective-permute-start | bytes 1572872 | tf_op jit(solution)/shard_map/ppermute | solution.py:292
  60.9 2.4 %collective-permute-start.1 = (bf16[32,64,128]{2,1,0:T(8,128)(2,1)S(1)}, bf16[32,64,128]{2,1,0:T(8,128)(2,1)S(1)}, u32[]{:S(2)}, u32[]{:S(2)}) collective-permute-start(bf16[32,64,128]{2,1,0:T(8,128)(2,1)S(1)} %shard_map.60.state), channel_id=1, source_target_pairs={{0,1},{1,0},{2,3},{3,2},{4,5},{5,4},{6,7},{7,6},{8,9},{9,8},{10,11... | collective-permute-start | bytes 1572872 | tf_op jit(solution)/shard_map/ppermute | solution.py:292
  65.4 18.9 %copy-start.1 = (bf16[128,4096]{1,0:T(8,128)(2,1)S(1)}, bf16[128,4096]{1,0:T(8,128)(2,1)}, u32[]{:S(2)}) copy-start(bf16[128,4096]{1,0:T(8,128)(2,1)} %maps.3) | copy-start | bytes 3145732

commit v4 on v3

--- a/solution.py
+++ b/solution.py
@@ -13,7 +13,7 @@
 WIDE = 2 * VECS
 TILES = 64
 AXES = ("yh", "x", "yl", "z", "core")
-CHIPS = ("yh", "x", "yl", "z")
+CHIPS = ("z", "x", "yh", "yl")
 
 
 def left_half(shape):
@@ -159,8 +159,18 @@
         swapped[m] = swap_halves(near[m])
 
 
+def chip_order(tile):
+    col, row = tile >> 3, tile & 7
+    return (row & 3) * 16 + (col & 3) * 4 + (col >> 2) * 2 + (row >> 2)
+
+
+def lane_of(tile, half):
+    return (tile >> 3) * 16 + half * 8 + (tile & 7)
+
+
 def lookup(chosen_ref, level):
-    return lambda tile, half: chosen_ref[level, (tile >> 3) * 16 + half * 8 + (tile & 7)]
+    row = chosen_ref[level : level + 1, :]
+    return lambda tile, half: row[0, lane_of(tile, half)]
 
 
 def first_kernel(chosen_ref, state, near, swapped, out, one, two):
@@ -170,7 +180,11 @@
         tile_level(
             getter(bufs[level]), setter(bufs[level + 1]), near, swapped, lookup(chosen_ref, level), bit, every
         )
-    lane_level(getter(two), setter(out), near, lookup(chosen_ref, 6), every)
+
+    def store(tile, value):
+        out[chip_order(tile)] = value
+
+    lane_level(getter(two), store, near, lookup(chosen_ref, 6), every)
 
 
 HALVES = [[tile for tile in range(TILES) if tile >> 2 & 1 == n] for n in range(2)]
@@ -186,7 +200,7 @@
     def store_out(tile, value):
         out[packed(tile)] = value
 
-    loads = [getter(state), getter(one), getter(two)]
+    loads = [lambda tile: state[chip_order(tile)], getter(one), getter(two)]
     stores = [setter(one), setter(two), store_out]
     for level in range(3):
         tile_level(
@@ -242,7 +256,6 @@
 
 
 VM = pl.BlockSpec(memory_space=pltpu.VMEM)
-SM = pl.BlockSpec(memory_space=pltpu.SMEM)
 HB = pl.BlockSpec(memory_space=pltpu.HBM)
 PARAMS = pltpu.CompilerParams(vmem_limit_bytes=32 * 1024 * 1024)
 STATE = jax.ShapeDtypeStruct((TILES, RANK, WIDE), jnp.bfloat16)
@@ -277,7 +290,7 @@
     first_chosen, second_chosen, near, swapped = make_tables(patterns, translations)
     state = lax.all_to_all(state, ("yh", "x"), 0, 0, tiled=True)
     state = pl.pallas_call(
-        first_kernel, out_shape=STATE, in_specs=[SM, VM, VM, VM], out_specs=VM,
+        first_kernel, out_shape=STATE, in_specs=[VM, VM, VM, VM], out_specs=VM,
         scratch_shapes=scratch, compiler_params=PARAMS,
     )(first_chosen, state, near, swapped)
     state = lax.all_to_all(state, CHIPS, 0, 0, tiled=True)
@@ -285,17 +298,17 @@
     for n in range(2):
         parts.append(
             pl.pallas_call(
-                functools.partial(second_kernel, n), out_shape=HALF, in_specs=[SM, VM, VM, VM], out_specs=VM,
+                functools.partial(second_kernel, n), out_shape=HALF, in_specs=[VM, VM, VM, VM], out_specs=VM,
                 scratch_shapes=scratch, compiler_params=PARAMS,
             )(second_chosen, state, near, swapped)
         )
         partners.append(lax.ppermute(parts[n], "core", [(0, 1), (1, 0)]))
     earlier = pl.pallas_call(
-        third_kernel, out_shape=HALF, in_specs=[SM, VM, VM, VM, VM], out_specs=VM,
+        third_kernel, out_shape=HALF, in_specs=[VM, VM, VM, VM, VM], out_specs=VM,
         scratch_shapes=scratch, compiler_params=PARAMS,
     )(second_chosen, parts[0], partners[0], near, swapped)
     state = pl.pallas_call(
-        fourth_kernel, out_shape=STATE, in_specs=[SM, VM, VM, VM, VM, VM], out_specs=VM,
+        fourth_kernel, out_shape=STATE, in_specs=[VM, VM, VM, VM, VM, VM], out_specs=VM,
         scratch_shapes=scratch, compiler_params=PARAMS,
     )(second_chosen, earlier, parts[1], partners[1], near, swapped)
     state = lax.all_to_all(state, ("yl", "z"), 0, 0, tiled=True)

time: 86.7 us -> 85.4 us (0.985)
  Pallas kernels: 17.6 us -> 16 us
  transfers between devices with their start and end apart: 3 -> 3, of which waited for: 1 -> 2; matrix products, arithmetic and copies ran while one was open for 1% -> 1% of each run, Pallas kernels for 5% -> 4%
where the time goes in v4:
time: 85.4 us; the launch traced here: 85.1 us
  blocking collectives  44.1 us (52%)
  Pallas kernels  16 us (19%)
  waiting for transfers between devices  13.3 us (16%)
  starting transfers between devices  7.87 us (9%)
  local copies, waits for them, and re-layouts  3.44 us (4%)
    all_to_all x1, blocking collectives, local(): state = lax.all_to_all(state, CHIPS, 0, 0, tiled=True)  25.4 us
    all_to_all x1, blocking collectives, local(): state = lax.all_to_all(state, ('yl', 'z'), 0, 0, tiled=True)  18.7 us
    all_to_all x1, waiting for transfers between devices, local(): state = lax.all_to_all(state, ('yh', 'x'), 0, 0, tiled=True)  13 us
    all_to_all x1, starting transfers between devices, local(): state = lax.all_to_all(state, ('yh', 'x'), 0, 0, tiled=True)  7.03 us
    pallas_call x1, Pallas kernels, local(): pl.pallas_call(first_kernel, out_shape=STATE, in_specs=[VM, VM, VM, VM],...  4.72 us
    pallas_call x1, Pallas kernels, local(): pl.pallas_call(leaf_kernel, out_shape=STATE, in_specs=[HB] * 2, out_specs...  3.36 us
    unnamed x6, local copies, waits for them, and re-layouts  2.45 us
    pallas_call x2, Pallas kernels, local(): pl.pallas_call(functools.partial(second_kernel, n), out_shape=HALF, in_sp...  2.41 us
  transfers between devices with their start and end apart: 3, of which 2 were waited for; matrix products, arithmetic and copies ran while one was open for 1% of the time, Pallas kernels for 4%

profile of v4, /device:TPU:0, one launch (start us, length us, event | category | flops | bytes accessed | tf_op | source)
XLA Modules:
  0.0 85.1 jit_solution(12270926664177872931)
XLA Ops:
  0.0 3.4 %shard_map.56 = bf16[64,64,128]{2,1,0:T(8,128)(2,1)} custom-call(bf16[128,4096]{1,0:T(8,128)(2,1)} %maps.2, bf16[128,4096]{1,0:T(8,128)(2,1)} %vectors.1), custom_call_target="tpu_custom_call" | custom-call | tf_op jit(solution)/shard_map/pallas_call | solution.py:284
  3.4 7.0 %all-to-all-start = ((bf16[64,64,128]{2,1,0:T(8,128)(2,1)}), bf16[64,64,128]{2,1,0:T(8,128)(2,1)S(1)}, u32[]{:S(2)}, u32[]{:S(2)}) async-start(bf16[64,64,128]{2,1,0:T(8,128)(2,1)} %shard_map.56), calls=%async_computation | async-start | bytes 2097152 | tf_op jit(solution)/shard_map/all_to_all | solution.py:291
  10.4 1.0 %constant_dynamic-slice_fusion.late_patterns = s32[8,2048]{1,0:T(8,128)S(1)} fusion(s32[14,16384]{1,0:T(8,128)} %patterns.1, s32[]{:T(128)S(6)} %select_n.3), kind=kLoop, calls=%fused_computation | loop fusion | bytes 131076 | tf_op jit(solution)/shard_map/dynamic_slice | solution.py:266
  11.4 0.0 copy-start
  11.4 1.2 %copy-done = s32[14,16384]{1,0:T(8,128)S(1)} copy-done((s32[14,16384]{1,0:T(8,128)S(1)}, s32[14,16384]{1,0:T(8,128)}, u32[]{:S(2)}) %copy-start) | copy-done | bytes 917528
  12.6 0.0 copy-start.2
  12.6 1.2 %copy-done.2 = bf16[64,64,128]{2,1,0:T(8,128)(2,1)S(1)} copy-done((bf16[64,64,128]{2,1,0:T(8,128)(2,1)S(1)}, bf16[64,64,128]{2,1,0:T(8,128)(2,1)}, u32[]{:S(2)}) %copy-start.2) | copy-done | bytes 1048600
  13.8 0.8 shard_map.55
  14.6 13.0 %all-to-all-done.state = bf16[64,64,128]{2,1,0:T(8,128)(2,1)S(1)} async-done(((bf16[64,64,128]{2,1,0:T(8,128)(2,1)}), bf16[64,64,128]{2,1,0:T(8,128)(2,1)S(1)}, u32[]{:S(2)}, u32[]{:S(2)}) %all-to-all-start) | async-done | bytes 1048608 | tf_op jit(solution)/shard_map/all_to_all | solution.py:291
  27.6 4.7 %shard_map.57 = bf16[64,64,128]{2,1,0:T(8,128)(2,1)S(1)} custom-call(s32[8,128]{1,0:T(8,128)S(1)} %get-tuple-element.10.chosen_ref, bf16[64,64,128]{2,1,0:T(8,128)(2,1)S(1)} %all-to-all-done.state, bf16[64,64,128]{2,1,0:T(8,128)(2,1)S(1)} %get-tuple-element.11.near, bf16[64,64,128]{2,1,0:T(8,128)(2,1)S(1)} %get-tuple-element.12.swapped), custom_call_target="tpu_custom_call" | custom-call | tf_op jit(solution)/shard_map/pallas_call | solution.py:292
  32.3 25.4 %all_to_all.15.state = bf16[64,64,128]{2,1,0:T(8,128)(2,1)S(1)} all-to-all(bf16[64,64,128]{2,1,0:T(8,128)(2,1)S(1)} %shard_map.57), channel_id=1, replica_groups=mesh['yh'=2,'x'=4,'yl'=2,'z'=4,'core'=2] {'z','x','yh','yl'}, dimensions={0} | all-to-all | bytes 2097152 | tf_op jit(solution)/shard_map/all_to_all | solution.py:296
  57.7 1.2 %shard_map.58.state = bf16[32,64,128]{2,1,0:T(8,128)(2,1)S(1)} custom-call(s32[8,128]{1,0:T(8,128)S(1)} %get-tuple-element.9.chosen_ref, bf16[64,64,128]{2,1,0:T(8,128)(2,1)S(1)} %all_to_all.15.state, bf16[64,64,128]{2,1,0:T(8,128)(2,1)S(1)} %get-tuple-element.11.near, bf16[64,64,128]{2,1,0:T(8,128)(2,1)S(1)} %get-tuple-element.12.swapped), custom_call_target="tpu_custom_call" | custom-call | tf_op jit(solution)/shard_map/pallas_call | solution.py:300
  59.0 0.1 collective-permute-start
  59.0 1.2 %shard_map.60.state = bf16[32,64,128]{2,1,0:T(8,128)(2,1)S(1)} custom-call(s32[8,128]{1,0:T(8,128)S(1)} %get-tuple-element.9.chosen_ref, bf16[64,64,128]{2,1,0:T(8,128)(2,1)S(1)} %all_to_all.15.state, bf16[64,64,128]{2,1,0:T(8,128)(2,1)S(1)} %get-tuple-element.11.near, bf16[64,64,128]{2,1,0:T(8,128)(2,1)S(1)} %get-tuple-element.12.swapped), custom_call_target="tpu_custom_call" | custom-call | tf_op jit(solution)/shard_map/pallas_call | solution.py:300
  60.2 0.8 collective-permute-start.1
  61.0 0.0 collective-permute-done.partner
  61.0 1.2 %shard_map.59.earlier = bf16[32,64,128]{2,1,0:T(8,128)(2,1)S(1)} custom-call(s32[8,128]{1,0:T(8,128)S(1)} %get-tuple-element.9.chosen_ref, bf16[32,64,128]{2,1,0:T(8,128)(2,1)S(1)} %shard_map.58.state, bf16[32,64,128]{2,1,0:T(8,128)(2,1)S(1)} %collective-permute-done.partner, bf16[64,64,128]{2,1,0:T(8,128)(2,1)S(1)} %get-tuple-element.11.near, ...), custom_call_target="tpu_custom_call" | custom-call | tf_op jit(solution)/shard_map/pallas_call | solution.py:306
  62.2 0.4 collective-permute-done.1.partner
  62.5 1.8 %shard_map.61 = bf16[64,64,128]{2,1,0:T(8,128)(2,1)S(1)} custom-call(s32[8,128]{1,0:T(8,128)S(1)} %get-tuple-element.9.chosen_ref, bf16[32,64,128]{2,1,0:T(8,128)(2,1)S(1)} %shard_map.59.earlier, bf16[32,64,128]{2,1,0:T(8,128)(2,1)S(1)} %shard_map.60.state, bf16[32,64,128]{2,1,0:T(8,128)(2,1)S(1)} %collective-permute-done.1.partner, ...), custom_call_target="tpu_custom_call" | custom-call | tf_op jit(solution)/shard_map/pallas_call | solution.py:310
  64.4 0.0 copy-start.1
  64.4 18.7 %all_to_all.16.state = bf16[64,64,128]{2,1,0:T(8,128)(2,1)S(1)} all-to-all(bf16[64,64,128]{2,1,0:T(8,128)(2,1)S(1)} %shard_map.61), channel_id=1, replica_groups=mesh['yh'=2,'x'=4,'yl'=2,'z'=4,'core'=2] {'yl','z'}, dimensions={0} | all-to-all | bytes 2097152 | tf_op jit(solution)/shard_map/all_to_all | solution.py:314
  83.1 0.0 copy-done.1
  83.1 1.8 %shard_map.62 = bf16[128,4096]{1,0:T(8,128)(2,1)} custom-call(bf16[64,64,128]{2,1,0:T(8,128)(2,1)S(1)} %all_to_all.16.state, bf16[128,4096]{1,0:T(8,128)(2,1)S(1)} %copy-done.1), custom_call_target="tpu_custom_call" | custom-call | tf_op jit(solution)/shard_map/pallas_call | solution.py:315
Async XLA Ops:
  3.4 24.2 %all-to-all-start = ((bf16[64,64,128]{2,1,0:T(8,128)(2,1)}), bf16[64,64,128]{2,1,0:T(8,128)(2,1)S(1)}, u32[]{:S(2)}, u32[]{:S(2)}) async-start(bf16[64,64,128]{2,1,0:T(8,128)(2,1)} %shard_map.56), calls=%async_computation | async-start | bytes 2097152 | tf_op jit(solution)/shard_map/all_to_all | solution.py:291
  11.4 1.2 %copy-start = (s32[14,16384]{1,0:T(8,128)S(1)}, s32[14,16384]{1,0:T(8,128)}, u32[]{:S(2)}) copy-start(s32[14,16384]{1,0:T(8,128)} %patterns.1) | copy-start | bytes 2752516
  12.6 1.2 %copy-start.2 = (bf16[64,64,128]{2,1,0:T(8,128)(2,1)S(1)}, bf16[64,64,128]{2,1,0:T(8,128)(2,1)}, u32[]{:S(2)}) copy-start(bf16[64,64,128]{2,1,0:T(8,128)(2,1)} %translations.1) | copy-start | bytes 3145732
  59.0 2.1 %collective-permute-start = (bf16[32,64,128]{2,1,0:T(8,128)(2,1)S(1)}, bf16[32,64,128]{2,1,0:T(8,128)(2,1)S(1)}, u32[]{:S(2)}, u32[]{:S(2)}) collective-permute-start(bf16[32,64,128]{2,1,0:T(8,128)(2,1)S(1)} %shard_map.58.state), channel_id=1, source_target_pairs={{0,1},{1,0},{2,3},{3,2},{4,5},{5,4},{6,7},{7,6},{8,9},{9,8},{10,11... | collective-permute-start | bytes 1572872 | tf_op jit(solution)/shard_map/ppermute | solution.py:305
  60.2 2.3 %collective-permute-start.1 = (bf16[32,64,128]{2,1,0:T(8,128)(2,1)S(1)}, bf16[32,64,128]{2,1,0:T(8,128)(2,1)S(1)}, u32[]{:S(2)}, u32[]{:S(2)}) collective-permute-start(bf16[32,64,128]{2,1,0:T(8,128)(2,1)S(1)} %shard_map.60.state), channel_id=1, source_target_pairs={{0,1},{1,0},{2,3},{3,2},{4,5},{5,4},{6,7},{7,6},{8,9},{9,8},{10,11... | collective-permute-start | bytes 1572872 | tf_op jit(solution)/shard_map/ppermute | solution.py:305
  64.4 18.7 %copy-start.1 = (bf16[128,4096]{1,0:T(8,128)(2,1)S(1)}, bf16[128,4096]{1,0:T(8,128)(2,1)}, u32[]{:S(2)}) copy-start(bf16[128,4096]{1,0:T(8,128)(2,1)} %maps.3) | copy-start | bytes 3145732

commit v5 on v4

--- a/solution.py
+++ b/solution.py
@@ -13,7 +13,7 @@
 WIDE = 2 * VECS
 TILES = 64
 AXES = ("yh", "x", "yl", "z", "core")
-CHIPS = ("z", "x", "yh", "yl")
+CHIPS = ("x", "z", "yh", "yl")
 
 
 def left_half(shape):
@@ -161,7 +161,7 @@
 
 def chip_order(tile):
     col, row = tile >> 3, tile & 7
-    return (row & 3) * 16 + (col & 3) * 4 + (col >> 2) * 2 + (row >> 2)
+    return (col & 3) * 16 + (row & 3) * 4 + (col >> 2) * 2 + (row >> 2)
 
 
 def lane_of(tile, half):
@@ -173,18 +173,24 @@
     return lambda tile, half: row[0, lane_of(tile, half)]
 
 
-def first_kernel(chosen_ref, state, near, swapped, out, one, two):
+def first_kernel(chosen_ref, state, near, swapped, out, one, two, spread):
+    for level in range(7):
+        spread[level] = jnp.broadcast_to(chosen_ref[level : level + 1, :], (128, 128)).T
+
+    def lookup(level):
+        return lambda tile, half: spread[level, lane_of(tile, half) : lane_of(tile, half) + 1, :][0, 0]
+
     every = range(TILES)
     bufs = [state, one, two, one, two, one, two]
     for level, bit in enumerate((3, 4, 5, 0, 1, 2)):
         tile_level(
-            getter(bufs[level]), setter(bufs[level + 1]), near, swapped, lookup(chosen_ref, level), bit, every
+            getter(bufs[level]), setter(bufs[level + 1]), near, swapped, lookup(level), bit, every
         )
 
     def store(tile, value):
         out[chip_order(tile)] = value
 
-    lane_level(getter(two), store, near, lookup(chosen_ref, 6), every)
+    lane_level(getter(two), store, near, lookup(6), every)
 
 
 HALVES = [[tile for tile in range(TILES) if tile >> 2 & 1 == n] for n in range(2)]
@@ -291,7 +297,7 @@
     state = lax.all_to_all(state, ("yh", "x"), 0, 0, tiled=True)
     state = pl.pallas_call(
         first_kernel, out_shape=STATE, in_specs=[VM, VM, VM, VM], out_specs=VM,
-        scratch_shapes=scratch, compiler_params=PARAMS,
+        scratch_shapes=scratch + [pltpu.VMEM((7, 128, 128), jnp.int32)], compiler_params=PARAMS,
     )(first_chosen, state, near, swapped)
     state = lax.all_to_all(state, CHIPS, 0, 0, tiled=True)
     parts, partners = [], []

time: 85.4 us -> 85.1 us (level)
  no operation moved by 1% of the time
where the time goes in v5:
time: 85.1 us; the launch traced here: 84.8 us
  blocking collectives  44 us (52%)
  Pallas kernels  15.9 us (19%)
  waiting for transfers between devices  13.3 us (16%)
  starting transfers between devices  7.87 us (9%)
  local copies, waits for them, and re-layouts  3.44 us (4%)
    all_to_all x1, blocking collectives, local(): state = lax.all_to_all(state, CHIPS, 0, 0, tiled=True)  25.2 us
    all_to_all x1, blocking collectives, local(): state = lax.all_to_all(state, ('yl', 'z'), 0, 0, tiled=True)  18.7 us
    all_to_all x1, waiting for transfers between devices, local(): state = lax.all_to_all(state, ('yh', 'x'), 0, 0, tiled=True)  13 us
    all_to_all x1, starting transfers between devices, local(): state = lax.all_to_all(state, ('yh', 'x'), 0, 0, tiled=True)  7.03 us
    pallas_call x1, Pallas kernels, local(): pl.pallas_call(first_kernel, out_shape=STATE, in_specs=[VM, VM, VM, VM],...  4.6 us
    pallas_call x1, Pallas kernels, local(): pl.pallas_call(leaf_kernel, out_shape=STATE, in_specs=[HB] * 2, out_specs...  3.36 us
    unnamed x6, local copies, waits for them, and re-layouts  2.45 us
    pallas_call x2, Pallas kernels, local(): pl.pallas_call(functools.partial(second_kernel, n), out_shape=HALF, in_sp...  2.41 us
  transfers between devices with their start and end apart: 3, of which 2 were waited for; matrix products, arithmetic and copies ran while one was open for 1% of the time, Pallas kernels for 4%

profile of v5, /device:TPU:0, one launch (start us, length us, event | category | flops | bytes accessed | tf_op | source)
XLA Modules:
  0.0 84.8 jit_solution(14627863586191213031)
XLA Ops:
  0.0 3.4 %shard_map.56 = bf16[64,64,128]{2,1,0:T(8,128)(2,1)} custom-call(bf16[128,4096]{1,0:T(8,128)(2,1)} %maps.2, bf16[128,4096]{1,0:T(8,128)(2,1)} %vectors.1), custom_call_target="tpu_custom_call" | custom-call | tf_op jit(solution)/shard_map/pallas_call | solution.py:290
  3.4 7.0 %all-to-all-start = ((bf16[64,64,128]{2,1,0:T(8,128)(2,1)}), bf16[64,64,128]{2,1,0:T(8,128)(2,1)S(1)}, u32[]{:S(2)}, u32[]{:S(2)}) async-start(bf16[64,64,128]{2,1,0:T(8,128)(2,1)} %shard_map.56), calls=%async_computation | async-start | bytes 2097152 | tf_op jit(solution)/shard_map/all_to_all | solution.py:297
  10.4 1.0 %constant_dynamic-slice_fusion.late_patterns = s32[8,2048]{1,0:T(8,128)S(1)} fusion(s32[14,16384]{1,0:T(8,128)} %patterns.1, s32[]{:T(128)S(6)} %select_n.3), kind=kLoop, calls=%fused_computation | loop fusion | bytes 131076 | tf_op jit(solution)/shard_map/dynamic_slice | solution.py:272
  11.4 0.0 copy-start
  11.4 1.2 %copy-done = s32[14,16384]{1,0:T(8,128)S(1)} copy-done((s32[14,16384]{1,0:T(8,128)S(1)}, s32[14,16384]{1,0:T(8,128)}, u32[]{:S(2)}) %copy-start) | copy-done | bytes 917528
  12.6 0.0 copy-start.2
  12.6 1.2 %copy-done.2 = bf16[64,64,128]{2,1,0:T(8,128)(2,1)S(1)} copy-done((bf16[64,64,128]{2,1,0:T(8,128)(2,1)S(1)}, bf16[64,64,128]{2,1,0:T(8,128)(2,1)}, u32[]{:S(2)}) %copy-start.2) | copy-done | bytes 1048600
  13.8 0.8 shard_map.55
  14.6 13.0 %all-to-all-done.state = bf16[64,64,128]{2,1,0:T(8,128)(2,1)S(1)} async-done(((bf16[64,64,128]{2,1,0:T(8,128)(2,1)}), bf16[64,64,128]{2,1,0:T(8,128)(2,1)S(1)}, u32[]{:S(2)}, u32[]{:S(2)}) %all-to-all-start) | async-done | bytes 1048608 | tf_op jit(solution)/shard_map/all_to_all | solution.py:297
  27.6 4.6 %shard_map.57 = bf16[64,64,128]{2,1,0:T(8,128)(2,1)S(1)} custom-call(s32[8,128]{1,0:T(8,128)S(1)} %get-tuple-element.10.chosen_ref, bf16[64,64,128]{2,1,0:T(8,128)(2,1)S(1)} %all-to-all-done.state, bf16[64,64,128]{2,1,0:T(8,128)(2,1)S(1)} %get-tuple-element.11.near, bf16[64,64,128]{2,1,0:T(8,128)(2,1)S(1)} %get-tuple-element.12.swapped), custom_call_target="tpu_custom_call" | custom-call | tf_op jit(solution)/shard_map/pallas_call | solution.py:298
  32.2 25.2 %all_to_all.15.state = bf16[64,64,128]{2,1,0:T(8,128)(2,1)S(1)} all-to-all(bf16[64,64,128]{2,1,0:T(8,128)(2,1)S(1)} %shard_map.57), channel_id=1, replica_groups=mesh['yh'=2,'x'=4,'yl'=2,'z'=4,'core'=2] {'x','z','yh','yl'}, dimensions={0} | all-to-all | bytes 2097152 | tf_op jit(solution)/shard_map/all_to_all | solution.py:302
  57.4 1.2 %shard_map.58.state = bf16[32,64,128]{2,1,0:T(8,128)(2,1)S(1)} custom-call(s32[8,128]{1,0:T(8,128)S(1)} %get-tuple-element.9.chosen_ref, bf16[64,64,128]{2,1,0:T(8,128)(2,1)S(1)} %all_to_all.15.state, bf16[64,64,128]{2,1,0:T(8,128)(2,1)S(1)} %get-tuple-element.11.near, bf16[64,64,128]{2,1,0:T(8,128)(2,1)S(1)} %get-tuple-element.12.swapped), custom_call_target="tpu_custom_call" | custom-call | tf_op jit(solution)/shard_map/pallas_call | solution.py:306
  58.7 0.1 collective-permute-start
  58.7 1.2 %shard_map.60.state = bf16[32,64,128]{2,1,0:T(8,128)(2,1)S(1)} custom-call(s32[8,128]{1,0:T(8,128)S(1)} %get-tuple-element.9.chosen_ref, bf16[64,64,128]{2,1,0:T(8,128)(2,1)S(1)} %all_to_all.15.state, bf16[64,64,128]{2,1,0:T(8,128)(2,1)S(1)} %get-tuple-element.11.near, bf16[64,64,128]{2,1,0:T(8,128)(2,1)S(1)} %get-tuple-element.12.swapped), custom_call_target="tpu_custom_call" | custom-call | tf_op jit(solution)/shard_map/pallas_call | solution.py:306
  60.0 0.8 collective-permute-start.1
  60.7 0.0 collective-permute-done.partner
  60.7 1.2 %shard_map.59.earlier = bf16[32,64,128]{2,1,0:T(8,128)(2,1)S(1)} custom-call(s32[8,128]{1,0:T(8,128)S(1)} %get-tuple-element.9.chosen_ref, bf16[32,64,128]{2,1,0:T(8,128)(2,1)S(1)} %shard_map.58.state, bf16[32,64,128]{2,1,0:T(8,128)(2,1)S(1)} %collective-permute-done.partner, bf16[64,64,128]{2,1,0:T(8,128)(2,1)S(1)} %get-tuple-element.11.near, ...), custom_call_target="tpu_custom_call" | custom-call | tf_op jit(solution)/shard_map/pallas_call | solution.py:312
  61.9 0.4 collective-permute-done.1.partner
  62.2 1.8 %shard_map.61 = bf16[64,64,128]{2,1,0:T(8,128)(2,1)S(1)} custom-call(s32[8,128]{1,0:T(8,128)S(1)} %get-tuple-element.9.chosen_ref, bf16[32,64,128]{2,1,0:T(8,128)(2,1)S(1)} %shard_map.59.earlier, bf16[32,64,128]{2,1,0:T(8,128)(2,1)S(1)} %shard_map.60.state, bf16[32,64,128]{2,1,0:T(8,128)(2,1)S(1)} %collective-permute-done.1.partner, ...), custom_call_target="tpu_custom_call" | custom-call | tf_op jit(solution)/shard_map/pallas_call | solution.py:316
  64.1 0.0 copy-start.1
  64.1 18.7 %all_to_all.16.state = bf16[64,64,128]{2,1,0:T(8,128)(2,1)S(1)} all-to-all(bf16[64,64,128]{2,1,0:T(8,128)(2,1)S(1)} %shard_map.61), channel_id=1, replica_groups=mesh['yh'=2,'x'=4,'yl'=2,'z'=4,'core'=2] {'yl','z'}, dimensions={0} | all-to-all | bytes 2097152 | tf_op jit(solution)/shard_map/all_to_all | solution.py:320
  82.8 0.0 copy-done.1
  82.8 1.8 %shard_map.62 = bf16[128,4096]{1,0:T(8,128)(2,1)} custom-call(bf16[64,64,128]{2,1,0:T(8,128)(2,1)S(1)} %all_to_all.16.state, bf16[128,4096]{1,0:T(8,128)(2,1)S(1)} %copy-done.1), custom_call_target="tpu_custom_call" | custom-call | tf_op jit(solution)/shard_map/pallas_call | solution.py:321
Async XLA Ops:
  3.4 24.2 %all-to-all-start = ((bf16[64,64,128]{2,1,0:T(8,128)(2,1)}), bf16[64,64,128]{2,1,0:T(8,128)(2,1)S(1)}, u32[]{:S(2)}, u32[]{:S(2)}) async-start(bf16[64,64,128]{2,1,0:T(8,128)(2,1)} %shard_map.56), calls=%async_computation | async-start | bytes 2097152 | tf_op jit(solution)/shard_map/all_to_all | solution.py:297
  11.4 1.2 %copy-start = (s32[14,16384]{1,0:T(8,128)S(1)}, s32[14,16384]{1,0:T(8,128)}, u32[]{:S(2)}) copy-start(s32[14,16384]{1,0:T(8,128)} %patterns.1) | copy-start | bytes 2752516
  12.6 1.2 %copy-start.2 = (bf16[64,64,128]{2,1,0:T(8,128)(2,1)S(1)}, bf16[64,64,128]{2,1,0:T(8,128)(2,1)}, u32[]{:S(2)}) copy-start(bf16[64,64,128]{2,1,0:T(8,128)(2,1)} %translations.1) | copy-start | bytes 3145732
  58.7 2.1 %collective-permute-start = (bf16[32,64,128]{2,1,0:T(8,128)(2,1)S(1)}, bf16[32,64,128]{2,1,0:T(8,128)(2,1)S(1)}, u32[]{:S(2)}, u32[]{:S(2)}) collective-permute-start(bf16[32,64,128]{2,1,0:T(8,128)(2,1)S(1)} %shard_map.58.state), channel_id=1, source_target_pairs={{0,1},{1,0},{2,3},{3,2},{4,5},{5,4},{6,7},{7,6},{8,9},{9,8},{10,11... | collective-permute-start | bytes 1572872 | tf_op jit(solution)/shard_map/ppermute | solution.py:311
  60.0 2.3 %collective-permute-start.1 = (bf16[32,64,128]{2,1,0:T(8,128)(2,1)S(1)}, bf16[32,64,128]{2,1,0:T(8,128)(2,1)S(1)}, u32[]{:S(2)}, u32[]{:S(2)}) collective-permute-start(bf16[32,64,128]{2,1,0:T(8,128)(2,1)S(1)} %shard_map.60.state), channel_id=1, source_target_pairs={{0,1},{1,0},{2,3},{3,2},{4,5},{5,4},{6,7},{7,6},{8,9},{9,8},{10,11... | collective-permute-start | bytes 1572872 | tf_op jit(solution)/shard_map/ppermute | solution.py:311
  64.1 18.7 %copy-start.1 = (bf16[128,4096]{1,0:T(8,128)(2,1)S(1)}, bf16[128,4096]{1,0:T(8,128)(2,1)}, u32[]{:S(2)}) copy-start(bf16[128,4096]{1,0:T(8,128)(2,1)} %maps.3) | copy-start | bytes 3145732

commit v6 on v5

--- a/solution.py
+++ b/solution.py
@@ -13,7 +13,7 @@
 WIDE = 2 * VECS
 TILES = 64
 AXES = ("yh", "x", "yl", "z", "core")
-CHIPS = ("x", "z", "yh", "yl")
+CHIPS = ("z", "x", "yh", "yl")
 
 
 def left_half(shape):
@@ -161,7 +161,7 @@
 
 def chip_order(tile):
     col, row = tile >> 3, tile & 7
-    return (col & 3) * 16 + (row & 3) * 4 + (col >> 2) * 2 + (row >> 2)
+    return (row & 3) * 16 + (col & 3) * 4 + (col >> 2) * 2 + (row >> 2)
 
 
 def lane_of(tile, half):

time: 85.1 us -> 85.4 us (level)
  no operation moved by 1% of the time
where the time goes in v6:
time: 85.4 us; the launch traced here: 84.9 us
  blocking collectives  44.2 us (52%)
  Pallas kernels  15.9 us (19%)
  waiting for transfers between devices  13.3 us (16%)
  starting transfers between devices  7.87 us (9%)
  local copies, waits for them, and re-layouts  3.44 us (4%)
    all_to_all x1, blocking collectives, local(): state = lax.all_to_all(state, CHIPS, 0, 0, tiled=True)  25.4 us
    all_to_all x1, blocking collectives, local(): state = lax.all_to_all(state, ('yl', 'z'), 0, 0, tiled=True)  18.7 us
    all_to_all x1, waiting for transfers between devices, local(): state = lax.all_to_all(state, ('yh', 'x'), 0, 0, tiled=True)  13 us
    all_to_all x1, starting transfers between devices, local(): state = lax.all_to_all(state, ('yh', 'x'), 0, 0, tiled=True)  7.03 us
    pallas_call x1, Pallas kernels, local(): pl.pallas_call(first_kernel, out_shape=STATE, in_specs=[VM, VM, VM, VM],...  4.58 us
    pallas_call x1, Pallas kernels, local(): pl.pallas_call(leaf_kernel, out_shape=STATE, in_specs=[HB] * 2, out_specs...  3.36 us
    unnamed x6, local copies, waits for them, and re-layouts  2.45 us
    pallas_call x2, Pallas kernels, local(): pl.pallas_call(functools.partial(second_kernel, n), out_shape=HALF, in_sp...  2.41 us
  transfers between devices with their start and end apart: 3, of which 2 were waited for; matrix products, arithmetic and copies ran while one was open for 1% of the time, Pallas kernels for 4%

profile of v6, /device:TPU:0, one launch (start us, length us, event | category | flops | bytes accessed | tf_op | source)
XLA Modules:
  0.0 84.9 jit_solution(7354747988794281307)
XLA Ops:
  0.0 3.4 %shard_map.56 = bf16[64,64,128]{2,1,0:T(8,128)(2,1)} custom-call(bf16[128,4096]{1,0:T(8,128)(2,1)} %maps.2, bf16[128,4096]{1,0:T(8,128)(2,1)} %vectors.1), custom_call_target="tpu_custom_call" | custom-call | tf_op jit(solution)/shard_map/pallas_call | solution.py:290
  3.4 7.0 %all-to-all-start = ((bf16[64,64,128]{2,1,0:T(8,128)(2,1)}), bf16[64,64,128]{2,1,0:T(8,128)(2,1)S(1)}, u32[]{:S(2)}, u32[]{:S(2)}) async-start(bf16[64,64,128]{2,1,0:T(8,128)(2,1)} %shard_map.56), calls=%async_computation | async-start | bytes 2097152 | tf_op jit(solution)/shard_map/all_to_all | solution.py:297
  10.4 1.0 %constant_dynamic-slice_fusion.late_patterns = s32[8,2048]{1,0:T(8,128)S(1)} fusion(s32[14,16384]{1,0:T(8,128)} %patterns.1, s32[]{:T(128)S(6)} %select_n.3), kind=kLoop, calls=%fused_computation | loop fusion | bytes 131076 | tf_op jit(solution)/shard_map/dynamic_slice | solution.py:272
  11.4 0.0 copy-start
  11.4 1.2 %copy-done = s32[14,16384]{1,0:T(8,128)S(1)} copy-done((s32[14,16384]{1,0:T(8,128)S(1)}, s32[14,16384]{1,0:T(8,128)}, u32[]{:S(2)}) %copy-start) | copy-done | bytes 917528
  12.6 0.0 copy-start.2
  12.6 1.2 %copy-done.2 = bf16[64,64,128]{2,1,0:T(8,128)(2,1)S(1)} copy-done((bf16[64,64,128]{2,1,0:T(8,128)(2,1)S(1)}, bf16[64,64,128]{2,1,0:T(8,128)(2,1)}, u32[]{:S(2)}) %copy-start.2) | copy-done | bytes 1048600
  13.8 0.8 shard_map.55
  14.6 13.0 %all-to-all-done.state = bf16[64,64,128]{2,1,0:T(8,128)(2,1)S(1)} async-done(((bf16[64,64,128]{2,1,0:T(8,128)(2,1)}), bf16[64,64,128]{2,1,0:T(8,128)(2,1)S(1)}, u32[]{:S(2)}, u32[]{:S(2)}) %all-to-all-start) | async-done | bytes 1048608 | tf_op jit(solution)/shard_map/all_to_all | solution.py:297
  27.6 4.6 %shard_map.57 = bf16[64,64,128]{2,1,0:T(8,128)(2,1)S(1)} custom-call(s32[8,128]{1,0:T(8,128)S(1)} %get-tuple-element.10.chosen_ref, bf16[64,64,128]{2,1,0:T(8,128)(2,1)S(1)} %all-to-all-done.state, bf16[64,64,128]{2,1,0:T(8,128)(2,1)S(1)} %get-tuple-element.11.near, bf16[64,64,128]{2,1,0:T(8,128)(2,1)S(1)} %get-tuple-element.12.swapped), custom_call_target="tpu_custom_call" | custom-call | tf_op jit(solution)/shard_map/pallas_call | solution.py:298
  32.2 25.4 %all_to_all.15.state = bf16[64,64,128]{2,1,0:T(8,128)(2,1)S(1)} all-to-all(bf16[64,64,128]{2,1,0:T(8,128)(2,1)S(1)} %shard_map.57), channel_id=1, replica_groups=mesh['yh'=2,'x'=4,'yl'=2,'z'=4,'core'=2] {'z','x','yh','yl'}, dimensions={0} | all-to-all | bytes 2097152 | tf_op jit(solution)/shard_map/all_to_all | solution.py:302
  57.6 1.2 %shard_map.58.state = bf16[32,64,128]{2,1,0:T(8,128)(2,1)S(1)} custom-call(s32[8,128]{1,0:T(8,128)S(1)} %get-tuple-element.9.chosen_ref, bf16[64,64,128]{2,1,0:T(8,128)(2,1)S(1)} %all_to_all.15.state, bf16[64,64,128]{2,1,0:T(8,128)(2,1)S(1)} %get-tuple-element.11.near, bf16[64,64,128]{2,1,0:T(8,128)(2,1)S(1)} %get-tuple-element.12.swapped), custom_call_target="tpu_custom_call" | custom-call | tf_op jit(solution)/shard_map/pallas_call | solution.py:306
  58.8 0.1 collective-permute-start
  58.9 1.2 %shard_map.60.state = bf16[32,64,128]{2,1,0:T(8,128)(2,1)S(1)} custom-call(s32[8,128]{1,0:T(8,128)S(1)} %get-tuple-element.9.chosen_ref, bf16[64,64,128]{2,1,0:T(8,128)(2,1)S(1)} %all_to_all.15.state, bf16[64,64,128]{2,1,0:T(8,128)(2,1)S(1)} %get-tuple-element.11.near, bf16[64,64,128]{2,1,0:T(8,128)(2,1)S(1)} %get-tuple-element.12.swapped), custom_call_target="tpu_custom_call" | custom-call | tf_op jit(solution)/shard_map/pallas_call | solution.py:306
  60.1 0.8 collective-permute-start.1
  60.9 0.0 collective-permute-done.partner
  60.9 1.2 %shard_map.59.earlier = bf16[32,64,128]{2,1,0:T(8,128)(2,1)S(1)} custom-call(s32[8,128]{1,0:T(8,128)S(1)} %get-tuple-element.9.chosen_ref, bf16[32,64,128]{2,1,0:T(8,128)(2,1)S(1)} %shard_map.58.state, bf16[32,64,128]{2,1,0:T(8,128)(2,1)S(1)} %collective-permute-done.partner, bf16[64,64,128]{2,1,0:T(8,128)(2,1)S(1)} %get-tuple-element.11.near, ...), custom_call_target="tpu_custom_call" | custom-call | tf_op jit(solution)/shard_map/pallas_call | solution.py:312
  62.1 0.3 collective-permute-done.1.partner
  62.4 1.8 %shard_map.61 = bf16[64,64,128]{2,1,0:T(8,128)(2,1)S(1)} custom-call(s32[8,128]{1,0:T(8,128)S(1)} %get-tuple-element.9.chosen_ref, bf16[32,64,128]{2,1,0:T(8,128)(2,1)S(1)} %shard_map.59.earlier, bf16[32,64,128]{2,1,0:T(8,128)(2,1)S(1)} %shard_map.60.state, bf16[32,64,128]{2,1,0:T(8,128)(2,1)S(1)} %collective-permute-done.1.partner, ...), custom_call_target="tpu_custom_call" | custom-call | tf_op jit(solution)/shard_map/pallas_call | solution.py:316
  64.2 0.0 copy-start.1
  64.2 18.7 %all_to_all.16.state = bf16[64,64,128]{2,1,0:T(8,128)(2,1)S(1)} all-to-all(bf16[64,64,128]{2,1,0:T(8,128)(2,1)S(1)} %shard_map.61), channel_id=1, replica_groups=mesh['yh'=2,'x'=4,'yl'=2,'z'=4,'core'=2] {'yl','z'}, dimensions={0} | all-to-all | bytes 2097152 | tf_op jit(solution)/shard_map/all_to_all | solution.py:320
  83.0 0.0 copy-done.1
  83.0 1.8 %shard_map.62 = bf16[128,4096]{1,0:T(8,128)(2,1)} custom-call(bf16[64,64,128]{2,1,0:T(8,128)(2,1)S(1)} %all_to_all.16.state, bf16[128,4096]{1,0:T(8,128)(2,1)S(1)} %copy-done.1), custom_call_target="tpu_custom_call" | custom-call | tf_op jit(solution)/shard_map/pallas_call | solution.py:321
Async XLA Ops:
  3.4 24.2 %all-to-all-start = ((bf16[64,64,128]{2,1,0:T(8,128)(2,1)}), bf16[64,64,128]{2,1,0:T(8,128)(2,1)S(1)}, u32[]{:S(2)}, u32[]{:S(2)}) async-start(bf16[64,64,128]{2,1,0:T(8,128)(2,1)} %shard_map.56), calls=%async_computation | async-start | bytes 2097152 | tf_op jit(solution)/shard_map/all_to_all | solution.py:297
  11.4 1.2 %copy-start = (s32[14,16384]{1,0:T(8,128)S(1)}, s32[14,16384]{1,0:T(8,128)}, u32[]{:S(2)}) copy-start(s32[14,16384]{1,0:T(8,128)} %patterns.1) | copy-start | bytes 2752516
  12.6 1.2 %copy-start.2 = (bf16[64,64,128]{2,1,0:T(8,128)(2,1)S(1)}, bf16[64,64,128]{2,1,0:T(8,128)(2,1)}, u32[]{:S(2)}) copy-start(bf16[64,64,128]{2,1,0:T(8,128)(2,1)} %translations.1) | copy-start | bytes 3145732
  58.8 2.1 %collective-permute-start = (bf16[32,64,128]{2,1,0:T(8,128)(2,1)S(1)}, bf16[32,64,128]{2,1,0:T(8,128)(2,1)S(1)}, u32[]{:S(2)}, u32[]{:S(2)}) collective-permute-start(bf16[32,64,128]{2,1,0:T(8,128)(2,1)S(1)} %shard_map.58.state), channel_id=1, source_target_pairs={{0,1},{1,0},{2,3},{3,2},{4,5},{5,4},{6,7},{7,6},{8,9},{9,8},{10,11... | collective-permute-start | bytes 1572872 | tf_op jit(solution)/shard_map/ppermute | solution.py:311
  60.1 2.3 %collective-permute-start.1 = (bf16[32,64,128]{2,1,0:T(8,128)(2,1)S(1)}, bf16[32,64,128]{2,1,0:T(8,128)(2,1)S(1)}, u32[]{:S(2)}, u32[]{:S(2)}) collective-permute-start(bf16[32,64,128]{2,1,0:T(8,128)(2,1)S(1)} %shard_map.60.state), channel_id=1, source_target_pairs={{0,1},{1,0},{2,3},{3,2},{4,5},{5,4},{6,7},{7,6},{8,9},{9,8},{10,11... | collective-permute-start | bytes 1572872 | tf_op jit(solution)/shard_map/ppermute | solution.py:311
  64.2 18.7 %copy-start.1 = (bf16[128,4096]{1,0:T(8,128)(2,1)S(1)}, bf16[128,4096]{1,0:T(8,128)(2,1)}, u32[]{:S(2)}) copy-start(bf16[128,4096]{1,0:T(8,128)(2,1)} %maps.3) | copy-start | bytes 3145732

commit v7 on v4

--- a/solution.py
+++ b/solution.py
@@ -13,7 +13,7 @@
 WIDE = 2 * VECS
 TILES = 64
 AXES = ("yh", "x", "yl", "z", "core")
-CHIPS = ("z", "x", "yh", "yl")
+CHIPS = ("x", "z", "yh", "yl")
 
 
 def left_half(shape):
@@ -161,7 +161,7 @@
 
 def chip_order(tile):
     col, row = tile >> 3, tile & 7
-    return (row & 3) * 16 + (col & 3) * 4 + (col >> 2) * 2 + (row >> 2)
+    return (col & 3) * 16 + (row & 3) * 4 + (col >> 2) * 2 + (row >> 2)
 
 
 def lane_of(tile, half):

time: 85.4 us -> 85.3 us (level)
  no operation moved by 1% of the time
where the time goes in v7:
time: 85.3 us; the launch traced here: 84.9 us
  blocking collectives  44 us (52%)
  Pallas kernels  16 us (19%)
  waiting for transfers between devices  13.3 us (16%)
  starting transfers between devices  7.87 us (9%)
  local copies, waits for them, and re-layouts  3.44 us (4%)
    all_to_all x1, blocking collectives, local(): state = lax.all_to_all(state, CHIPS, 0, 0, tiled=True)  25.2 us
    all_to_all x1, blocking collectives, local(): state = lax.all_to_all(state, ('yl', 'z'), 0, 0, tiled=True)  18.7 us
    all_to_all x1, waiting for transfers between devices, local(): state = lax.all_to_all(state, ('yh', 'x'), 0, 0, tiled=True)  13 us
    all_to_all x1, starting transfers between devices, local(): state = lax.all_to_all(state, ('yh', 'x'), 0, 0, tiled=True)  7.03 us
    pallas_call x1, Pallas kernels, local(): pl.pallas_call(first_kernel, out_shape=STATE, in_specs=[VM, VM, VM, VM],...  4.72 us
    pallas_call x1, Pallas kernels, local(): pl.pallas_call(leaf_kernel, out_shape=STATE, in_specs=[HB] * 2, out_specs...  3.36 us
    unnamed x6, local copies, waits for them, and re-layouts  2.45 us
    pallas_call x2, Pallas kernels, local(): pl.pallas_call(functools.partial(second_kernel, n), out_shape=HALF, in_sp...  2.42 us
  transfers between devices with their start and end apart: 3, of which 2 were waited for; matrix products, arithmetic and copies ran while one was open for 1% of the time, Pallas kernels for 4%

profile of v7, /device:TPU:0, one launch (start us, length us, event | category | flops | bytes accessed | tf_op | source)
XLA Modules:
  0.0 84.9 jit_solution(7439953393583264441)
XLA Ops:
  0.0 3.4 %shard_map.56 = bf16[64,64,128]{2,1,0:T(8,128)(2,1)} custom-call(bf16[128,4096]{1,0:T(8,128)(2,1)} %maps.2, bf16[128,4096]{1,0:T(8,128)(2,1)} %vectors.1), custom_call_target="tpu_custom_call" | custom-call | tf_op jit(solution)/shard_map/pallas_call | solution.py:284
  3.4 7.0 %all-to-all-start = ((bf16[64,64,128]{2,1,0:T(8,128)(2,1)}), bf16[64,64,128]{2,1,0:T(8,128)(2,1)S(1)}, u32[]{:S(2)}, u32[]{:S(2)}) async-start(bf16[64,64,128]{2,1,0:T(8,128)(2,1)} %shard_map.56), calls=%async_computation | async-start | bytes 2097152 | tf_op jit(solution)/shard_map/all_to_all | solution.py:291
  10.4 1.0 %constant_dynamic-slice_fusion.late_patterns = s32[8,2048]{1,0:T(8,128)S(1)} fusion(s32[14,16384]{1,0:T(8,128)} %patterns.1, s32[]{:T(128)S(6)} %select_n.3), kind=kLoop, calls=%fused_computation | loop fusion | bytes 131076 | tf_op jit(solution)/shard_map/dynamic_slice | solution.py:266
  11.4 0.0 copy-start
  11.4 1.2 %copy-done = s32[14,16384]{1,0:T(8,128)S(1)} copy-done((s32[14,16384]{1,0:T(8,128)S(1)}, s32[14,16384]{1,0:T(8,128)}, u32[]{:S(2)}) %copy-start) | copy-done | bytes 917528
  12.6 0.0 copy-start.2
  12.6 1.2 %copy-done.2 = bf16[64,64,128]{2,1,0:T(8,128)(2,1)S(1)} copy-done((bf16[64,64,128]{2,1,0:T(8,128)(2,1)S(1)}, bf16[64,64,128]{2,1,0:T(8,128)(2,1)}, u32[]{:S(2)}) %copy-start.2) | copy-done | bytes 1048600
  13.8 0.8 shard_map.55
  14.6 13.0 %all-to-all-done.state = bf16[64,64,128]{2,1,0:T(8,128)(2,1)S(1)} async-done(((bf16[64,64,128]{2,1,0:T(8,128)(2,1)}), bf16[64,64,128]{2,1,0:T(8,128)(2,1)S(1)}, u32[]{:S(2)}, u32[]{:S(2)}) %all-to-all-start) | async-done | bytes 1048608 | tf_op jit(solution)/shard_map/all_to_all | solution.py:291
  27.6 4.7 %shard_map.57 = bf16[64,64,128]{2,1,0:T(8,128)(2,1)S(1)} custom-call(s32[8,128]{1,0:T(8,128)S(1)} %get-tuple-element.10.chosen_ref, bf16[64,64,128]{2,1,0:T(8,128)(2,1)S(1)} %all-to-all-done.state, bf16[64,64,128]{2,1,0:T(8,128)(2,1)S(1)} %get-tuple-element.11.near, bf16[64,64,128]{2,1,0:T(8,128)(2,1)S(1)} %get-tuple-element.12.swapped), custom_call_target="tpu_custom_call" | custom-call | tf_op jit(solution)/shard_map/pallas_call | solution.py:292
  32.3 25.2 %all_to_all.15.state = bf16[64,64,128]{2,1,0:T(8,128)(2,1)S(1)} all-to-all(bf16[64,64,128]{2,1,0:T(8,128)(2,1)S(1)} %shard_map.57), channel_id=1, replica_groups=mesh['yh'=2,'x'=4,'yl'=2,'z'=4,'core'=2] {'x','z','yh','yl'}, dimensions={0} | all-to-all | bytes 2097152 | tf_op jit(solution)/shard_map/all_to_all | solution.py:296
  57.6 1.2 %shard_map.58.state = bf16[32,64,128]{2,1,0:T(8,128)(2,1)S(1)} custom-call(s32[8,128]{1,0:T(8,128)S(1)} %get-tuple-element.9.chosen_ref, bf16[64,64,128]{2,1,0:T(8,128)(2,1)S(1)} %all_to_all.15.state, bf16[64,64,128]{2,1,0:T(8,128)(2,1)S(1)} %get-tuple-element.11.near, bf16[64,64,128]{2,1,0:T(8,128)(2,1)S(1)} %get-tuple-element.12.swapped), custom_call_target="tpu_custom_call" | custom-call | tf_op jit(solution)/shard_map/pallas_call | solution.py:300
  58.8 0.1 collective-permute-start
  58.9 1.2 %shard_map.60.state = bf16[32,64,128]{2,1,0:T(8,128)(2,1)S(1)} custom-call(s32[8,128]{1,0:T(8,128)S(1)} %get-tuple-element.9.chosen_ref, bf16[64,64,128]{2,1,0:T(8,128)(2,1)S(1)} %all_to_all.15.state, bf16[64,64,128]{2,1,0:T(8,128)(2,1)S(1)} %get-tuple-element.11.near, bf16[64,64,128]{2,1,0:T(8,128)(2,1)S(1)} %get-tuple-element.12.swapped), custom_call_target="tpu_custom_call" | custom-call | tf_op jit(solution)/shard_map/pallas_call | solution.py:300
  60.1 0.8 collective-permute-start.1
  60.8 0.0 collective-permute-done.partner
  60.8 1.2 %shard_map.59.earlier = bf16[32,64,128]{2,1,0:T(8,128)(2,1)S(1)} custom-call(s32[8,128]{1,0:T(8,128)S(1)} %get-tuple-element.9.chosen_ref, bf16[32,64,128]{2,1,0:T(8,128)(2,1)S(1)} %shard_map.58.state, bf16[32,64,128]{2,1,0:T(8,128)(2,1)S(1)} %collective-permute-done.partner, bf16[64,64,128]{2,1,0:T(8,128)(2,1)S(1)} %get-tuple-element.11.near, ...), custom_call_target="tpu_custom_call" | custom-call | tf_op jit(solution)/shard_map/pallas_call | solution.py:306
  62.0 0.4 collective-permute-done.1.partner
  62.4 1.8 %shard_map.61 = bf16[64,64,128]{2,1,0:T(8,128)(2,1)S(1)} custom-call(s32[8,128]{1,0:T(8,128)S(1)} %get-tuple-element.9.chosen_ref, bf16[32,64,128]{2,1,0:T(8,128)(2,1)S(1)} %shard_map.59.earlier, bf16[32,64,128]{2,1,0:T(8,128)(2,1)S(1)} %shard_map.60.state, bf16[32,64,128]{2,1,0:T(8,128)(2,1)S(1)} %collective-permute-done.1.partner, ...), custom_call_target="tpu_custom_call" | custom-call | tf_op jit(solution)/shard_map/pallas_call | solution.py:310
  64.2 0.0 copy-start.1
  64.2 18.7 %all_to_all.16.state = bf16[64,64,128]{2,1,0:T(8,128)(2,1)S(1)} all-to-all(bf16[64,64,128]{2,1,0:T(8,128)(2,1)S(1)} %shard_map.61), channel_id=1, replica_groups=mesh['yh'=2,'x'=4,'yl'=2,'z'=4,'core'=2] {'yl','z'}, dimensions={0} | all-to-all | bytes 2097152 | tf_op jit(solution)/shard_map/all_to_all | solution.py:314
  82.9 0.0 copy-done.1
  82.9 1.8 %shard_map.62 = bf16[128,4096]{1,0:T(8,128)(2,1)} custom-call(bf16[64,64,128]{2,1,0:T(8,128)(2,1)S(1)} %all_to_all.16.state, bf16[128,4096]{1,0:T(8,128)(2,1)S(1)} %copy-done.1), custom_call_target="tpu_custom_call" | custom-call | tf_op jit(solution)/shard_map/pallas_call | solution.py:315
Async XLA Ops:
  3.4 24.2 %all-to-all-start = ((bf16[64,64,128]{2,1,0:T(8,128)(2,1)}), bf16[64,64,128]{2,1,0:T(8,128)(2,1)S(1)}, u32[]{:S(2)}, u32[]{:S(2)}) async-start(bf16[64,64,128]{2,1,0:T(8,128)(2,1)} %shard_map.56), calls=%async_computation | async-start | bytes 2097152 | tf_op jit(solution)/shard_map/all_to_all | solution.py:291
  11.4 1.2 %copy-start = (s32[14,16384]{1,0:T(8,128)S(1)}, s32[14,16384]{1,0:T(8,128)}, u32[]{:S(2)}) copy-start(s32[14,16384]{1,0:T(8,128)} %patterns.1) | copy-start | bytes 2752516
  12.6 1.2 %copy-start.2 = (bf16[64,64,128]{2,1,0:T(8,128)(2,1)S(1)}, bf16[64,64,128]{2,1,0:T(8,128)(2,1)}, u32[]{:S(2)}) copy-start(bf16[64,64,128]{2,1,0:T(8,128)(2,1)} %translations.1) | copy-start | bytes 3145732
  58.8 2.1 %collective-permute-start = (bf16[32,64,128]{2,1,0:T(8,128)(2,1)S(1)}, bf16[32,64,128]{2,1,0:T(8,128)(2,1)S(1)}, u32[]{:S(2)}, u32[]{:S(2)}) collective-permute-start(bf16[32,64,128]{2,1,0:T(8,128)(2,1)S(1)} %shard_map.58.state), channel_id=1, source_target_pairs={{0,1},{1,0},{2,3},{3,2},{4,5},{5,4},{6,7},{7,6},{8,9},{9,8},{10,11... | collective-permute-start | bytes 1572872 | tf_op jit(solution)/shard_map/ppermute | solution.py:305
  60.1 2.3 %collective-permute-start.1 = (bf16[32,64,128]{2,1,0:T(8,128)(2,1)S(1)}, bf16[32,64,128]{2,1,0:T(8,128)(2,1)S(1)}, u32[]{:S(2)}, u32[]{:S(2)}) collective-permute-start(bf16[32,64,128]{2,1,0:T(8,128)(2,1)S(1)} %shard_map.60.state), channel_id=1, source_target_pairs={{0,1},{1,0},{2,3},{3,2},{4,5},{5,4},{6,7},{7,6},{8,9},{9,8},{10,11... | collective-permute-start | bytes 1572872 | tf_op jit(solution)/shard_map/ppermute | solution.py:305
  64.2 18.7 %copy-start.1 = (bf16[128,4096]{1,0:T(8,128)(2,1)S(1)}, bf16[128,4096]{1,0:T(8,128)(2,1)}, u32[]{:S(2)}) copy-start(bf16[128,4096]{1,0:T(8,128)(2,1)} %maps.3) | copy-start | bytes 3145732
